TPU v7x, 768 devices: a whole 4x8x12 slice. The times are simulated.
768 devices in a mesh: occ: 12 (over z), tens: 64 (over y, x, core).
Axes of the slice: x: 4, y: 8, z: 12, core: 2. Of those that a mesh axis runs over, the one named last changes fastest.
Arguments:
- tensor: bfloat16 [512, 768, 768], P('tens'), may hold values from -6 to 6
- occ_green: bfloat16 [768, 768], P('occ'), may hold values from -0.21875 to 0.21875
- virt_green: bfloat16 [768, 768], replicated, may hold values from -0.21875 to 0.21875
- tensor_mask: int32 [12, 12], replicated, may hold values from 0 to 1, as said below
- occ_mask: int32 [12, 12], replicated, may hold values from 0 to 1, as said below
- virt_mask: int32 [12, 12], replicated, may hold values from 0 to 1, as said below
Outputs:
- chi: float32 [512, 512], P('tens')
Inputs may be any that keep to these rules, and one draw needn't show every extreme that they name: `tensor_mask`: 1 keeps the 64 x 64 block, 0 zeroes it; diagonal blocks are always kept. `occ_mask`: 1 keeps the 64 x 64 block, 0 zeroes it; diagonal blocks are always kept. `virt_mask`: 1 keeps the 64 x 64 block, 0 zeroes it; diagonal blocks are always kept.
All inputs are finite; a program needn't handle non-finite values.
Results may differ from a plain program's by a relative error of at most 0.0041.
Values may be sent and summed in bfloat16 or wider, within the bound.
No kernel may reach another device: no remote copies, remote signals or barrier semaphores. Data moves between devices by JAX's collectives and lax.ppermute only.
A program may use at most 64 MiB of HBM per device.

v0:
```python
import jax
import jax.numpy as jnp
from jax import lax
from jax.sharding import PartitionSpec as P

BLOCK = 64


def expand(pattern, block_width):
    return jnp.repeat(jnp.repeat(pattern, block_width, axis=0), block_width, axis=1)


def body(tensor, occ_green, virt_green, tensor_mask, occ_mask, virt_mask):
    rows_batch = occ_green.shape[0]
    ao_count = occ_green.shape[1]
    local_ri = tensor.shape[0]
    occ_index = lax.axis_index("occ")
    first_row = occ_index * rows_batch
    tensor_keep = expand(tensor_mask, BLOCK).astype(jnp.bfloat16)
    masked = tensor * tensor_keep[None]
    tensor_slab = lax.dynamic_slice_in_dim(masked, first_row, rows_batch, 1)
    tensor_slab = tensor_slab.reshape(local_ri, rows_batch * ao_count)
    moved_rows = lax.all_to_all(tensor_slab, "tens", split_axis=1, concat_axis=0, tiled=True)
    row_blocks = lax.dynamic_slice_in_dim(
        jnp.repeat(occ_mask, BLOCK, axis=0), first_row, rows_batch, 0
    )
    occ_keep = jnp.repeat(row_blocks, BLOCK, axis=1).astype(jnp.bfloat16)
    occ_part = occ_green * occ_keep
    virt_part = virt_green * expand(virt_mask, BLOCK).astype(jnp.bfloat16)
    occ_half = jnp.einsum(
        "im,pmn->pin", occ_part, masked, preferred_element_type=jnp.float32
    ).astype(jnp.bfloat16)
    screened = jnp.dot(
        occ_half.reshape(local_ri * rows_batch, ao_count),
        virt_part,
        preferred_element_type=jnp.float32,
    ).astype(jnp.bfloat16)
    moved_screened = lax.all_to_all(
        screened.reshape(local_ri, rows_batch * ao_count),
        "tens",
        split_axis=1,
        concat_axis=0,
        tiled=True,
    )
    partial_value = lax.dot_general(
        moved_screened, moved_rows, (((1,), (1,)), ((), ())), preferred_element_type=jnp.float32
    )
    chi_total = lax.psum(partial_value, "occ")
    chi_share = lax.psum_scatter(chi_total, "tens", scatter_dimension=0, tiled=True)
    return -chi_share / ao_count


def solution(mesh):
    in_specs = (P("tens", None, None), P("occ", None), P(), P(), P(), P())
    out_specs = P("tens", None)
    return jax.shard_map(body, mesh=mesh, in_specs=in_specs, out_specs=out_specs, check_vma=False)
```

profile of v0, /device:TPU:2, one launch (start us, length us, event | category | flops | bytes accessed | tf_op | source)
XLA Modules:
  0.0 350.8 jit_solution(17717079917169073633)
XLA Ops:
  6.5 0.7 convert_element_type.42
  7.2 0.1 copy.14
  7.3 0.1 broadcast_in_dim.19
  7.4 0.1 convert_element_type.43
  7.5 0.1 broadcast_in_dim.20
  7.6 0.6 copy.15
  8.3 14.0 %copy_multiply_fusion = bf16[8,768,768]{2,0,1:T(8,128)(2,1)} fusion(bf16[8,768,768]{2,1,0:T(8,128)(2,1)} %param.6, bf16[768,768]{1,0:T(8,128)(2,1)S(1)} %copy.15), kind=kLoop, calls=%fused_computation.2 | loop fusion | flops 4718592 | bytes 20054016 | tf_op jit(solution)/shard_map/mul | solution.py:20
  22.3 2.1 constant_dynamic-slice_fusion.1
  24.4 13.8 %all-to-all-start.1 = ((bf16[8,64,768]{2,0,1:T(8,128)(2,1)}), bf16[8,64,768]{2,0,1:T(8,128)(2,1)S(1)}, u32[]{:S(2)}, u32[]{:S(2)}) async-start(bf16[8,64,768]{2,0,1:T(8,128)(2,1)} %constant_dynamic-slice_fusion.1), calls=%async_computation.1 | async-start | bytes 1572864 | tf_op jit(solution)/shard_map/all_to_all | solution.py:23
  38.2 0.0 all-reduce.3.cloned.1.call-start
  38.3 0.0 copy-start.2
  38.3 0.2 broadcast_in_dim.22
  38.5 0.2 convert_element_type.46
  38.7 0.6 copy.19
  39.3 0.0 copy-start.3
  39.4 0.1 copy.18
  39.5 0.1 broadcast_in_dim.23
  39.6 0.1 convert_element_type.50
  39.7 0.1 bitcast_multiply_fusion
  39.8 0.5 copy-done.3
  40.2 6.7 %fusion.2 = bf16[8,768,64]{1,2,0:T(8,128)(2,1)S(1)} fusion(bf16[8,768,768]{2,0,1:T(8,128)(2,1)} %copy_multiply_fusion, bf16[64,768]{1,0:T(8,128)(2,1)S(1)} %copy-done.3, bf16[64,768]{1,0:T(8,128)(2,1)S(1)} %convert_element_type.46), kind=kOutput, calls=%fused_computation.4 | convolution fusion | flops 604569600 | bytes 10420224 | tf_op jit(solution)/shard_map/im,pmn->pin/dot_general | solution.py:30
  46.9 0.8 convolution_convert_fusion
  47.8 0.4 copy.20
  48.2 13.2 %all-to-all-done.1 = bf16[8,64,768]{2,0,1:T(8,128)(2,1)S(1)} async-done(((bf16[8,64,768]{2,0,1:T(8,128)(2,1)}), bf16[8,64,768]{2,0,1:T(8,128)(2,1)S(1)}, u32[]{:S(2)}, u32[]{:S(2)}) %all-to-all-start.1) | async-done | bytes 786464 | tf_op jit(solution)/shard_map/all_to_all | solution.py:23
  61.4 28.8 %all_to_all.35 = bf16[8,64,768]{2,0,1:T(8,128)(2,1)S(1)} all-to-all(bf16[8,64,768]{2,0,1:T(8,128)(2,1)S(1)} %copy.20), channel_id=1, replica_groups=mesh['occ'=12,'tens'=64] {'tens'}, dimensions={1} | all-to-all | bytes 1572864 | tf_op jit(solution)/shard_map/all_to_all | solution.py:38
  90.2 1.6 fusion.5
  91.8 0.0 all-reduce.3.cloned.1.call-update
  91.9 1.3 dynamic-slice
  93.8 204.4 %all-reduce.3.cloned.1.call-done = f32[512,512]{1,0:T(8,128)} async-done(((f32[512,512]{1,0:T(8,128)}), f32[512,512]{1,0:T(8,128)}) %all-reduce.3.cloned.1.call-update) | async-done | bytes 1048592
  298.2 0.7 constant_dynamic-slice_fusion
  298.9 44.4 %psum.8 = f32[8,512]{1,0:T(8,128)S(1)} all-reduce(f32[8,512]{1,0:T(8,128)S(1)} %constant_dynamic-slice_fusion), channel_id=1, replica_groups=mesh['occ'=12,'tens'=64] {'occ'}, use_global_device_ids=true, to_apply=%region_0.0 | all-reduce | flops 4096 | bytes 32768 | tf_op jit(solution)/shard_map/psum | solution.py:48
  343.3 0.6 negate_multiply_fusion
  (8 shorter events, 0.1 us)
Async XLA Ops:
  22.3 15.9 %copy-start.1 = (s32[12,12]{1,0:T(8,128)S(1)}, s32[12,12]{1,0:T(8,128)}, u32[]{:S(2)}) copy-start(s32[12,12]{1,0:T(8,128)} %param.10) | copy-start | bytes 1732
  24.4 14.3 %copy-start = (bf16[768,768]{1,0:T(8,128)(2,1)S(1)}, bf16[768,768]{1,0:T(8,128)(2,1)}, u32[]{:S(2)}) copy-start(bf16[768,768]{1,0:T(8,128)(2,1)} %param.8) | copy-start | bytes 3538948
  24.4 37.0 %all-to-all-start.1 = ((bf16[8,64,768]{2,0,1:T(8,128)(2,1)}), bf16[8,64,768]{2,0,1:T(8,128)(2,1)S(1)}, u32[]{:S(2)}, u32[]{:S(2)}) async-start(bf16[8,64,768]{2,0,1:T(8,128)(2,1)} %constant_dynamic-slice_fusion.1), calls=%async_computation.1 | async-start | bytes 1572864 | tf_op jit(solution)/shard_map/all_to_all | solution.py:23
  38.2 260.0 %all-reduce.3.cloned.1.call-start = ((), (), s32[]{:S(2)}) async-start(), calls=%async_computation.2 | async-start | bytes 2097152
  38.3 1.1 copy-start.2
  39.3 0.9 copy-start.3
Sparse Core Ops, SparseCore 0:
  92.0 206.1 all-reduce.2
where the time goes:
time: 351 us
  waiting for transfers between devices  218 us (62%)
  blocking collectives  73.2 us (21%)
  other arithmetic  15.4 us (4%)
  between operations  14.2 us (4%)
  starting transfers between devices  13.8 us (4%)
  matrix products  9.13 us (3%)
  local copies, waits for them, and re-layouts  7.35 us (2%)
    unnamed x2, waiting for transfers between devices  204 us
    psum x1, blocking collectives, body(): chi_total = lax.psum(partial_value, 'occ')  44.4 us
    all_to_all x1, blocking collectives, body(): lax.all_to_all(screened.reshape(local_ri, rows_batch * ao_count), 'tens',...  28.8 us
    mul x1, other arithmetic, body(): masked = tensor * tensor_keep[None]  14 us
    all_to_all x1, starting transfers between devices, body(): lax.all_to_all(tensor_slab, 'tens', split_axis=1, concat_axis=0, tiled=True)  13.8 us
    all_to_all x1, waiting for transfers between devices, body(): lax.all_to_all(tensor_slab, 'tens', split_axis=1, concat_axis=0, tiled=True)  13.2 us
  transfers between devices with their start and end apart: 2, of which 2 were waited for; matrix products, arithmetic and copies ran while one was open for 3% of the time, Pallas kernels for 0%

commit v1 on v0

v1 whole, which is shorter than its diff:
```python
import jax
import jax.numpy as jnp
from jax import lax
from jax.sharding import PartitionSpec as P

BLOCK = 64


def expand(pattern, block_width):
    return jnp.repeat(jnp.repeat(pattern, block_width, axis=0), block_width, axis=1)


def body(tensor, occ_green, virt_green, tensor_mask, occ_mask, virt_mask):
    rows_batch, ao_count = occ_green.shape
    local_ri = tensor.shape[0]
    batches = lax.axis_size("occ")
    cells = lax.axis_size("tens")
    chips = cells // 2
    same_core = [[2 * chip + core for chip in range(chips)] for core in range(2)]
    other_core = [(cell, cell ^ 1) for cell in range(cells)]
    bf16 = jnp.bfloat16
    occ_index = lax.axis_index("occ")
    core = lax.axis_index("tens") % 2
    first_row = occ_index * rows_batch
    per_chip = rows_batch * ao_count // chips

    def regroup(rows):
        message = rows.reshape(local_ri, chips, per_chip).transpose(1, 0, 2)
        moved = lax.all_to_all(
            message, "tens", 0, 0, axis_index_groups=same_core, tiled=True
        )
        return moved.reshape(chips * local_ri, per_chip)

    rows = lax.dynamic_slice_in_dim(tensor, first_row, rows_batch, 1)
    row_pattern = lax.dynamic_slice_in_dim(tensor_mask, occ_index, 1, 0)[0]
    rows = rows * jnp.repeat(row_pattern, BLOCK).astype(bf16)[None, None]
    with jax.named_scope("rows"):
        moved_rows = regroup(rows)

    masked = tensor * expand(tensor_mask, BLOCK).astype(bf16)[None]
    occ_pattern = lax.dynamic_slice_in_dim(occ_mask, occ_index, 1, 0)[0]
    occ_part = occ_green * jnp.repeat(occ_pattern, BLOCK).astype(bf16)[None]
    virt_part = virt_green * expand(virt_mask, BLOCK).astype(bf16)
    occ_half = jnp.einsum(
        "im,pmn->pin", occ_part, masked, preferred_element_type=jnp.float32
    ).astype(bf16)
    screened = jnp.dot(
        occ_half.reshape(local_ri * rows_batch, ao_count),
        virt_part,
        preferred_element_type=jnp.float32,
    ).astype(bf16)
    with jax.named_scope("other_rows"):
        sibling_rows = lax.ppermute(moved_rows, "tens", other_core)
    with jax.named_scope("screened"):
        moved_screened = regroup(screened.reshape(local_ri, rows_batch, ao_count))
    own = moved_rows.reshape(chips, 1, local_ri, per_chip)
    other = sibling_rows.reshape(chips, 1, local_ri, per_chip)
    first = jnp.where(core == 0, own, other)
    second = jnp.where(core == 0, other, own)
    all_rows = jnp.concatenate([first, second], axis=1).reshape(2 * chips * local_ri, per_chip)
    partial_value = lax.dot_general(
        moved_screened, all_rows, (((1,), (1,)), ((), ())), preferred_element_type=jnp.float32
    ).astype(bf16)
    with jax.named_scope("over_plane"):
        shares = lax.all_to_all(
            partial_value.reshape(chips, local_ri, -1),
            "tens",
            0,
            0,
            axis_index_groups=same_core,
            tiled=True,
        )
    batch_share = jnp.sum(shares.astype(jnp.float32), axis=0)
    copies = jnp.broadcast_to(batch_share[None], (batches,) + batch_share.shape)
    with jax.named_scope("over_batches"):
        batch_shares = lax.all_to_all(copies, "occ", 0, 0, tiled=True)
    return jnp.sum(batch_shares, axis=0) * (-1.0 / ao_count)


def solution(mesh):
    in_specs = (P("tens", None, None), P("occ", None), P(), P(), P(), P())
    out_specs = P("tens", None)
    return jax.shard_map(body, mesh=mesh, in_specs=in_specs, out_specs=out_specs, check_vma=False)
```

time: 351 us -> 116 us (0.33)
  the two profiles are of different devices: /device:TPU:2 before, /device:TPU:64 now
where the time goes in v1:
time: 116 us
  blocking collectives  44.1 us (38%)
  waiting for transfers between devices  34.6 us (30%)
  starting transfers between devices  16.9 us (15%)
  matrix products  9.31 us (8%)
  local copies, waits for them, and re-layouts  7.69 us (7%)
  other arithmetic  3 us (3%)
    all_to_all x2, waiting for transfers between devices, regroup(): lax.all_to_all(message, 'tens', 0, 0, axis_index_groups=same_core, tiled=...  34.6 us
    all_to_all x1, blocking collectives, body(): batch_shares = lax.all_to_all(copies, 'occ', 0, 0, tiled=True)  26.4 us
    all_to_all x1, blocking collectives, body(): lax.all_to_all(partial_value.reshape(chips, local_ri, -1), 'tens', 0, 0,...  17.7 us
    all_to_all x2, starting transfers between devices, regroup(): lax.all_to_all(message, 'tens', 0, 0, axis_index_groups=same_core, tiled=...  15 us
    dot_general x1, matrix products, body(): jnp.einsum('im,pmn->pin', occ_part, masked, preferred_element_type=jnp.fl...  6.77 us
  transfers between devices with their start and end apart: 3, of which 2 were waited for; matrix products, arithmetic and copies ran while one was open for 12% of the time, Pallas kernels for 0%

profile of v1, /device:TPU:64, one launch (start us, length us, event | category | flops | bytes accessed | tf_op | source)
XLA Modules:
  0.0 115.8 jit_solution(12698249195658815831)
XLA Ops:
  0.0 0.7 fusion.14
  0.8 0.1 convert_element_type.83
  0.9 1.3 %dynamic-slice_multiply_fusion = bf16[8,64,768]{2,1,0:T(8,128)(2,1)S(1)} fusion(bf16[8,768,768]{2,1,0:T(8,128)(2,1)} %param.6, s32[]{:T(128)S(6)} %select_n.35, bf16[768]{0:T(1024)(128)(2,1)S(1)} %convert_element_type.83), kind=kLoop, calls=%fused_computation.15 | loop fusion | flops 1572864 | bytes 1574404 | tf_op jit(solution)/shard_map/mul | solution.py:36
  2.1 0.3 reshape.62
  2.4 1.4 %copy.34 = bf16[32,8,1536]{2,1,0:T(8,128)(2,1)} copy(bf16[32,8,1536]{2,0,1:T(8,128)(2,1)S(1)} %bitcast.43) | data formatting | bytes 1572864 | tf_op jit(solution)/shard_map/rows/transpose | solution.py:28
  3.8 10.0 %all-to-all-start.1 = ((bf16[32,8,1536]{2,1,0:T(8,128)(2,1)}), bf16[32,8,1536]{2,1,0:T(8,128)(2,1)S(1)}, u32[]{:S(2)}, u32[]{:S(2)}) async-start(bf16[32,8,1536]{2,1,0:T(8,128)(2,1)} %copy.34), calls=%async_computation.1 | async-start | bytes 1572864 | tf_op jit(solution)/shard_map/rows/all_to_all | solution.py:29
  13.9 0.1 convert_element_type.74
  14.0 0.1 copy.31
  14.1 0.1 copy.29
  14.2 0.1 broadcast_in_dim.27
  14.3 0.1 convert_element_type.70
  14.4 0.1 broadcast_in_dim.30
  14.5 0.1 convert_element_type.78
  14.7 1.5 %copy.30 = bf16[768,768]{1,0:T(8,128)(2,1)} copy(bf16[768,768]{0,1:T(8,128)(2,1)S(1)} %bitcast.42) | data formatting | bytes 2359296 | tf_op jit(solution)/shard_map/convert_element_type | solution.py:40
  16.2 0.6 copy.32
  16.8 0.1 bitcast_multiply_fusion
  16.9 1.2 copy-done.1
  18.1 6.8 %fusion.3 = bf16[8,768,64]{1,2,0:T(8,128)(2,1)} fusion(bf16[8,768,768]{2,1,0:T(8,128)(2,1)} %param.6, bf16[768,768]{1,0:T(8,128)(2,1)S(1)} %copy-done.1, bf16[64,768]{1,0:T(8,128)(2,1)S(1)} %copy-done.4, bf16[768]{0:T(1024)(128)(2,1)S(1)} %convert_element_type.74), kind=kOutput, calls=%fused_computation.5 | convolution fusion | flops 623443968 | bytes 11503104 | tf_op jit(solution)/shard_map/im,pmn->pin/dot_general | solution.py:44
  24.8 11.9 %all-to-all-done.1 = bf16[32,8,1536]{2,1,0:T(8,128)(2,1)S(1)} async-done(((bf16[32,8,1536]{2,1,0:T(8,128)(2,1)}), bf16[32,8,1536]{2,1,0:T(8,128)(2,1)S(1)}, u32[]{:S(2)}, u32[]{:S(2)}) %all-to-all-start.1) | async-done | bytes 786464 | tf_op jit(solution)/shard_map/rows/all_to_all | solution.py:29
  36.7 1.9 %collective-permute-start = (bf16[256,1536]{1,0:T(8,128)(2,1)S(1)}, bf16[256,1536]{1,0:T(8,128)(2,1)S(1)}, u32[]{:S(2)}, u32[]{:S(2)}) collective-permute-start(bf16[256,1536]{1,0:T(8,128)(2,1)S(1)} %bitcast.44), channel_id=1, source_target_pairs={{0,1},{1,0},{2,3},{3,2},{4,5},{5,4},{6,7},{7,6},{8,9},{9,8},{10,11... | collective-permute-start | bytes 2359304 | tf_op jit(solution)/shard_map/other_rows/ppermute | solution.py:53
  38.6 1.9 %convolution_convert_fusion = bf16[512,768]{1,0:T(8,128)(2,1)S(1)} fusion(bf16[512,768]{1,0:T(8,128)(2,1)} %bitcast.46, bf16[768,768]{0,1:T(8,128)(2,1)S(1)} %bitcast_multiply_fusion), kind=kOutput, calls=%fused_computation.4 | convolution fusion | flops 604372992 | bytes 2752512 | tf_op jit(solution)/shard_map/dot_general | solution.py:47
  40.6 0.3 reshape.60
  40.8 1.3 %copy.37 = bf16[8,32,1536]{2,0,1:T(8,128)(2,1)} copy(bf16[8,32,1536]{2,1,0:T(8,128)(2,1)S(1)} %reshape.60) | data formatting | bytes 1572864 | tf_op jit(solution)/shard_map/screened/reshape;screened/reshape | solution.py:28
  42.2 5.1 %all-to-all-start = ((bf16[32,8,1536]{2,1,0:T(8,128)(2,1)}), bf16[32,8,1536]{2,1,0:T(8,128)(2,1)S(1)}, u32[]{:S(2)}, u32[]{:S(2)}) async-start(bf16[32,8,1536]{2,1,0:T(8,128)(2,1)} %bitcast.41), calls=%async_computation | async-start | bytes 1572864 | tf_op jit(solution)/shard_map/screened/all_to_all | solution.py:29
  47.3 0.1 fusion.7
  47.4 0.1 pad_maximum_fusion
  47.6 0.2 copy.35
  47.7 22.7 %all-to-all-done = bf16[32,8,1536]{2,1,0:T(8,128)(2,1)S(1)} async-done(((bf16[32,8,1536]{2,1,0:T(8,128)(2,1)}), bf16[32,8,1536]{2,1,0:T(8,128)(2,1)S(1)}, u32[]{:S(2)}, u32[]{:S(2)}) %all-to-all-start) | async-done | bytes 786464 | tf_op jit(solution)/shard_map/screened/all_to_all | solution.py:29
  70.4 0.6 fusion.6
  71.0 17.7 %all_to_all.20 = bf16[32,8,512]{2,1,0:T(8,128)(2,1)S(1)} all-to-all(bf16[32,8,512]{2,1,0:T(8,128)(2,1)S(1)} %fusion.6), channel_id=1, replica_groups={{0,2,4,6,8,10,12,14,16,18,20,22,24,26,28,30,32,34,36,38,40,42,44,46,48,..., dimensions={0} | all-to-all | bytes 524288 | tf_op jit(solution)/shard_map/over_plane/all_to_all | solution.py:65
  88.8 26.4 %all_to_all.21 = f32[12,8,512]{2,1,0:T(8,128)S(1)} all-to-all(f32[12,8,512]{2,1,0:T(8,128)S(1)} %broadcast_in_dim.33), channel_id=1, replica_groups=mesh['occ'=12,'tens'=64] {'occ'}, dimensions={0} | all-to-all | bytes 393216 | tf_op jit(solution)/shard_map/over_batches/all_to_all | solution.py:76
  115.2 0.6 broadcast_multiply_fusion
  (18 shorter events, 0.3 us)
Async XLA Ops:
  2.4 11.4 %copy-start.2 = (s32[12,12]{1,0:T(8,128)S(1)}, s32[12,12]{1,0:T(8,128)}, u32[]{:S(2)}) copy-start(s32[12,12]{1,0:T(8,128)} %param.9) | copy-start | bytes 1732
  2.4 11.5 %copy-start.3 = (s32[12,12]{1,0:T(8,128)S(1)}, s32[12,12]{1,0:T(8,128)}, u32[]{:S(2)}) copy-start(s32[12,12]{1,0:T(8,128)} %param.11) | copy-start | bytes 1732
  3.8 32.9 %all-to-all-start.1 = ((bf16[32,8,1536]{2,1,0:T(8,128)(2,1)}), bf16[32,8,1536]{2,1,0:T(8,128)(2,1)S(1)}, u32[]{:S(2)}, u32[]{:S(2)}) async-start(bf16[32,8,1536]{2,1,0:T(8,128)(2,1)} %copy.34), calls=%async_computation.1 | async-start | bytes 1572864 | tf_op jit(solution)/shard_map/rows/all_to_all | solution.py:29
  14.6 1.6 %copy-start = (bf16[768,768]{1,0:T(8,128)(2,1)S(1)}, bf16[768,768]{1,0:T(8,128)(2,1)}, u32[]{:S(2)}) copy-start(bf16[768,768]{1,0:T(8,128)(2,1)} %param.8) | copy-start | bytes 3538948
  16.8 1.3 %copy-start.1 = (bf16[768,768]{1,0:T(8,128)(2,1)S(1)}, bf16[768,768]{1,0:T(8,128)(2,1)}, u32[]{:S(2)}) copy-start(bf16[768,768]{1,0:T(8,128)(2,1)} %copy.30) | copy-start | bytes 3538948
  16.8 1.3 %copy-start.4 = (bf16[64,768]{1,0:T(8,128)(2,1)S(1)}, bf16[64,768]{1,0:T(8,128)(2,1)}, u32[]{:S(2)}) copy-start(bf16[64,768]{1,0:T(8,128)(2,1)} %param.7) | copy-start | bytes 294916
  36.7 10.6 %collective-permute-start = (bf16[256,1536]{1,0:T(8,128)(2,1)S(1)}, bf16[256,1536]{1,0:T(8,128)(2,1)S(1)}, u32[]{:S(2)}, u32[]{:S(2)}) collective-permute-start(bf16[256,1536]{1,0:T(8,128)(2,1)S(1)} %bitcast.44), channel_id=1, source_target_pairs={{0,1},{1,0},{2,3},{3,2},{4,5},{5,4},{6,7},{7,6},{8,9},{9,8},{10,11... | collective-permute-start | bytes 2359304 | tf_op jit(solution)/shard_map/other_rows/ppermute | solution.py:53
  42.2 28.3 %all-to-all-start = ((bf16[32,8,1536]{2,1,0:T(8,128)(2,1)}), bf16[32,8,1536]{2,1,0:T(8,128)(2,1)S(1)}, u32[]{:S(2)}, u32[]{:S(2)}) async-start(bf16[32,8,1536]{2,1,0:T(8,128)(2,1)} %bitcast.41), calls=%async_computation | async-start | bytes 1572864 | tf_op jit(solution)/shard_map/screened/all_to_all | solution.py:29

commit v2 on v1

v2 whole, which is shorter than its diff:
```python
import jax
import jax.numpy as jnp
from jax import lax
from jax.experimental import pallas as pl
from jax.experimental.pallas import tpu as pltpu
from jax.sharding import PartitionSpec as P

BLOCK = 64
LANES = 128
BF16 = jnp.bfloat16
F32 = jnp.float32


def block_of(size, blocks):
    position = lax.broadcasted_iota(jnp.int32, (size, blocks), 0)
    start = lax.broadcasted_iota(jnp.int32, (size, blocks), 1) * BLOCK
    return ((position >= start) & (position < start + BLOCK)).astype(BF16)


def dot(a, b):
    return jnp.dot(a, b, preferred_element_type=F32)


def dot_t(a, b):
    return lax.dot_general(a, b, (((1,), (1,)), ((), ())), preferred_element_type=F32)


def as_bf16(pattern):
    return pattern.astype(F32).astype(BF16)


def spread(pattern, rows, columns):
    across = dot_t(as_bf16(pattern), block_of(columns, pattern.shape[1])).astype(BF16)
    return dot(block_of(rows, pattern.shape[0]), across).astype(BF16)


def place(staged, values, index, count):
    half, tiles = values.shape[0] // 2, values.shape[1] // LANES
    for tile in range(tiles):
        columns = values[:, tile * LANES : (tile + 1) * LANES]
        staged[tile, pl.ds(index, half, stride=count), :] = columns[:half]
        staged[tiles + tile, pl.ds(index, half, stride=count), :] = columns[half:]


def finish(staged, out_ref):
    for tile in range(staged.shape[0]):
        out_ref[:, tile * LANES : (tile + 1) * LANES] = staged[tile].astype(BF16)


def rows_kernel(batch_ref, tensor_ref, mask_ref, out_ref, staged):
    count, rows, columns = tensor_ref.shape
    pattern = as_bf16(mask_ref[pl.ds(batch_ref[0], 1), :])
    keep = dot_t(pattern, block_of(columns, pattern.shape[1]))
    for index in range(count):
        place(staged, tensor_ref[index].astype(F32) * keep, index, count)
    finish(staged, out_ref)


def screened_kernel(
    batch_ref, tensor_ref, occ_ref, virt_ref, tmask_ref, omask_ref, vmask_ref, out_ref,
    keep, occ_part, virt_part, staged,
):
    index, count = pl.program_id(0), pl.num_programs(0)
    ao_count = virt_ref.shape[0]

    @pl.when(index == 0)
    def _():
        keep[...] = spread(tmask_ref[...], ao_count, ao_count)
        virt_part[...] = virt_ref[...] * spread(vmask_ref[...], ao_count, ao_count)
        pattern = as_bf16(omask_ref[pl.ds(batch_ref[0], 1), :])
        row_keep = dot_t(pattern, block_of(ao_count, pattern.shape[1])).astype(BF16)
        occ_part[...] = occ_ref[...] * row_keep

    half = dot(occ_part[...], tensor_ref[0] * keep[...]).astype(BF16)
    values = dot(half, virt_part[...])
    place(staged, values, index, 8)

    @pl.when(index == count - 1)
    def _():
        finish(staged, out_ref)


def row_messages(batch, tensor, tensor_mask, rows):
    count, _, columns = tensor.shape
    shape = (rows // 2 * count, 2 * columns)
    return pl.pallas_call(
        rows_kernel,
        out_shape=jax.ShapeDtypeStruct(shape, BF16),
        grid_spec=pltpu.PrefetchScalarGridSpec(
            num_scalar_prefetch=1,
            grid=(1,),
            in_specs=[
                pl.BlockSpec((count, rows, columns), lambda s, batch: (0, batch[0], 0)),
                pl.BlockSpec(tensor_mask.shape, lambda s, batch: (0, 0)),
            ],
            out_specs=pl.BlockSpec(shape, lambda s, batch: (0, 0)),
            scratch_shapes=[pltpu.VMEM((shape[1] // LANES, shape[0], LANES), F32)],
        ),
        compiler_params=pltpu.CompilerParams(vmem_limit_bytes=16 * 2**20),
        name="row_messages",
    )(batch, tensor, tensor_mask)


def screened_messages(batch, tensor, occ_green, virt_green, tensor_mask, occ_mask, virt_mask):
    count, ao_count, _ = tensor.shape
    rows = occ_green.shape[0]
    shape = (rows // 2 * count, 2 * ao_count)
    whole = lambda s, batch: (0, 0)
    pattern = pl.BlockSpec(tensor_mask.shape, whole)
    work = count * rows * ao_count * ao_count
    return pl.pallas_call(
        screened_kernel,
        out_shape=jax.ShapeDtypeStruct(shape, BF16),
        grid_spec=pltpu.PrefetchScalarGridSpec(
            num_scalar_prefetch=1,
            grid=(count,),
            in_specs=[
                pl.BlockSpec((1, ao_count, ao_count), lambda s, batch: (s, 0, 0)),
                pl.BlockSpec(occ_green.shape, whole),
                pl.BlockSpec(virt_green.shape, whole),
                pattern,
                pattern,
                pattern,
            ],
            out_specs=pl.BlockSpec(shape, whole),
            scratch_shapes=[
                pltpu.VMEM((ao_count, ao_count), BF16),
                pltpu.VMEM(occ_green.shape, BF16),
                pltpu.VMEM(virt_green.shape, BF16),
                pltpu.VMEM((shape[1] // LANES, shape[0], LANES), F32),
            ],
        ),
        compiler_params=pltpu.CompilerParams(vmem_limit_bytes=28 * 2**20),
        cost_estimate=pl.CostEstimate(
            flops=4 * work, bytes_accessed=2 * tensor.size + 4 * virt_green.size, transcendentals=0
        ),
        name="screened_messages",
    )(batch, tensor, occ_green, virt_green, tensor_mask, occ_mask, virt_mask)


def body(tensor, occ_green, virt_green, tensor_mask, occ_mask, virt_mask):
    rows_batch, ao_count = occ_green.shape
    local_ri = tensor.shape[0]
    batches = lax.axis_size("occ")
    cells = lax.axis_size("tens")
    chips = cells // 2
    same_core = [[2 * chip + core for chip in range(chips)] for core in range(2)]
    other_core = [(cell, cell ^ 1) for cell in range(cells)]
    batch = lax.axis_index("occ").astype(jnp.int32).reshape(1)
    core = lax.axis_index("tens") % 2

    def over_plane(values):
        return lax.all_to_all(values, "tens", 0, 0, axis_index_groups=same_core, tiled=True)

    def regroup(messages):
        moved = over_plane(messages.reshape(chips, local_ri, -1))
        return moved.reshape(chips * local_ri, -1)

    messages = row_messages(batch, tensor, tensor_mask, rows_batch)
    with jax.named_scope("rows"):
        moved_rows = regroup(messages)
    screened = screened_messages(
        batch, tensor, occ_green, virt_green, tensor_mask, occ_mask, virt_mask
    )
    moved_rows, screened = lax.optimization_barrier((moved_rows, screened))
    with jax.named_scope("other_rows"):
        sibling_rows = lax.ppermute(moved_rows, "tens", other_core)
    with jax.named_scope("screened"):
        moved_screened = regroup(screened)
    own = moved_rows.reshape(chips, 1, local_ri, -1)
    other = sibling_rows.reshape(chips, 1, local_ri, -1)
    first = jnp.where(core == 0, own, other)
    second = jnp.where(core == 0, other, own)
    all_rows = jnp.concatenate([first, second], axis=1).reshape(2 * chips * local_ri, -1)
    partial_value = dot_t(moved_screened, all_rows).astype(BF16)
    with jax.named_scope("over_plane"):
        shares = over_plane(partial_value.reshape(chips, local_ri, -1))
    batch_share = jnp.sum(shares.astype(F32), axis=0)
    copies = jnp.broadcast_to(batch_share[None], (batches,) + batch_share.shape)
    with jax.named_scope("over_batches"):
        batch_shares = lax.all_to_all(copies, "occ", 0, 0, tiled=True)
    return jnp.sum(batch_shares, axis=0) * (-1.0 / ao_count)


def solution(mesh):
    in_specs = (P("tens", None, None), P("occ", None), P(), P(), P(), P())
    out_specs = P("tens", None)
    return jax.shard_map(body, mesh=mesh, in_specs=in_specs, out_specs=out_specs, check_vma=False)
```

time: 116 us -> 115 us (level)
  Pallas kernels: 0 us -> 8.95 us
  matrix products: 9.31 us -> 0.6 us
  other arithmetic: 3 us -> 0.92 us
    pallas_call x0 -> x2, Pallas kernels: none -> 8.95 us  [the longest x1 7.39 us: screened_messages(): pl.pallas_call(screened_kernel, out_shape=jax.ShapeDtypeStruct(shape, BF1...]
    dot_general x3 -> x1, matrix products: 9.31 us -> 0.6 us  [dot_t(): lax.dot_general(a, b, (((1,), (1,)), ((), ())), preferred_element_type=F32)]
    unnamed x11 -> x16, local copies, waits for them, and re-layouts: 1.82 us -> 8.07 us
    convert_element_type x7 -> x0, local copies, waits for them, and re-layouts: 2.03 us -> none  [the longest x3 1.66 us: body(): masked = tensor * expand(tensor_mask, BLOCK).astype(bf16)[None]]
    reshape x3 -> x0, local copies, waits for them, and re-layouts: 1.85 us -> none  [regroup(): message = rows.reshape(local_ri, chips, per_chip).transpose(1, 0, 2)]
    transpose x1 -> x0, local copies, waits for them, and re-layouts: 1.38 us -> none  [regroup(): message = rows.reshape(local_ri, chips, per_chip).transpose(1, 0, 2)]
    mul x2 -> x0, other arithmetic: 1.35 us -> none  [the longest x1 1.27 us: body(): rows = rows * jnp.repeat(row_pattern, BLOCK).astype(bf16)[None, None]]
  transfers between devices with their start and end apart: 3 -> 3, of which waited for: 2 -> 2; matrix products, arithmetic and copies ran while one was open for 12% -> 0% of each run, Pallas kernels for 0% -> 6%
where the time goes in v2:
time: 115 us
  blocking collectives  44.1 us (38%)
  waiting for transfers between devices  34.7 us (30%)
  starting transfers between devices  17.1 us (15%)
  Pallas kernels  8.95 us (8%)
  local copies, waits for them, and re-layouts  8.09 us (7%)
    all_to_all x2, waiting for transfers between devices, over_plane(): lax.all_to_all(values, 'tens', 0, 0, axis_index_groups=same_core, tiled=T...  34.7 us
    all_to_all x1, blocking collectives, body(): batch_shares = lax.all_to_all(copies, 'occ', 0, 0, tiled=True)  26.4 us
    all_to_all x1, blocking collectives, over_plane(): lax.all_to_all(values, 'tens', 0, 0, axis_index_groups=same_core, tiled=T...  17.7 us
    all_to_all x2, starting transfers between devices, over_plane(): lax.all_to_all(values, 'tens', 0, 0, axis_index_groups=same_core, tiled=T...  15.2 us
    unnamed x16, local copies, waits for them, and re-layouts  8.07 us
    pallas_call x1, Pallas kernels, screened_messages(): pl.pallas_call(screened_kernel, out_shape=jax.ShapeDtypeStruct(shape, BF1...  7.39 us
  transfers between devices with their start and end apart: 3, of which 2 were waited for; matrix products, arithmetic and copies ran while one was open for 0% of the time, Pallas kernels for 6%

profile of v2, /device:TPU:64, one launch (start us, length us, event | category | flops | bytes accessed | tf_op | source)
XLA Modules:
  0.0 114.6 jit_solution(2248167705541412929)
XLA Ops:
  0.0 0.0 copy-start
  0.0 3.7 %copy-done = bf16[8,768,768]{2,1,0:T(8,128)(2,1)S(1)} copy-done((bf16[8,768,768]{2,1,0:T(8,128)(2,1)S(1)}, bf16[8,768,768]{2,1,0:T(8,128)(2,1)}, u32[]{:S(2)}) %copy-start) | copy-done | bytes 9437208
  3.7 0.0 copy-start.4
  3.7 0.7 copy-done.4
  4.4 1.6 %row_messages.1 = bf16[256,1536]{1,0:T(8,128)(2,1)} custom-call(s32[1]{0:T(128)} %bitcast.batch_ref, bf16[8,768,768]{2,1,0:T(8,128)(2,1)S(1)} %copy-done, s32[12,12]{1,0:T(8,128)S(1)} %copy-done.4), custom_call_target="tpu_custom_call" | custom-call | tf_op jit(solution)/shard_map/row_messages/pallas_call | solution.py:86
  5.9 0.0 copy-start.2
  5.9 0.0 copy-start.3
  5.9 0.0 copy-start.5
  5.9 0.0 copy-start.6
  5.9 0.0 copy-start.7
  6.0 10.1 %all-to-all-start = ((bf16[32,8,1536]{2,1,0:T(8,128)(2,1)}), bf16[32,8,1536]{2,1,0:T(8,128)(2,1)S(1)}, u32[]{:S(2)}, u32[]{:S(2)}) async-start(bf16[32,8,1536]{2,1,0:T(8,128)(2,1)} %bitcast.1), calls=%async_computation | async-start | bytes 1572864 | tf_op jit(solution)/shard_map/rows/all_to_all | solution.py:153
  16.1 0.0 copy-done.2
  16.1 0.0 copy-done.3
  16.1 0.0 copy-done.5
  16.1 0.0 copy-done.6
  16.1 0.0 copy-done.7
  16.1 0.0 copy-start.1
  16.1 3.7 %copy-done.1 = bf16[8,768,768]{2,1,0:T(8,128)(2,1)S(1)} copy-done((bf16[8,768,768]{2,1,0:T(8,128)(2,1)S(1)}, bf16[8,768,768]{2,1,0:T(8,128)(2,1)}, u32[]{:S(2)}) %copy-start.1) | copy-done | bytes 9437208
  19.8 7.4 %screened_messages.1 = bf16[256,1536]{1,0:T(8,128)(2,1)} custom-call(s32[1]{0:T(128)} %bitcast.batch_ref, bf16[8,768,768]{2,1,0:T(8,128)(2,1)S(1)} %copy-done.1, bf16[64,768]{1,0:T(8,128)(2,1)S(1)} %copy-done.3, bf16[768,768]{1,0:T(8,128)(2,1)S(1)} %copy-done.2, s32[12,12]{1,0:T(8,128)S(1)} %copy-done.5, s32[12,12]{1,0:T(8,128)S(1)} %copy-done.6, ...), custom_call_target="tpu_custom_call" | custom-call | flops 1207959552 | bytes 11796480 | tf_op jit(solution)/shard_map/screened_messages/pallas_call | solution.py:111
  27.2 11.8 %all-to-all-done = bf16[32,8,1536]{2,1,0:T(8,128)(2,1)S(1)} async-done(((bf16[32,8,1536]{2,1,0:T(8,128)(2,1)}), bf16[32,8,1536]{2,1,0:T(8,128)(2,1)S(1)}, u32[]{:S(2)}, u32[]{:S(2)}) %all-to-all-start) | async-done | bytes 786464 | tf_op jit(solution)/shard_map/rows/all_to_all | solution.py:153
  39.0 1.9 %collective-permute-start = (bf16[256,1536]{1,0:T(8,128)(2,1)S(1)}, bf16[256,1536]{1,0:T(8,128)(2,1)S(1)}, u32[]{:S(2)}, u32[]{:S(2)}) collective-permute-start(bf16[256,1536]{1,0:T(8,128)(2,1)S(1)} %bitcast.15), channel_id=1, source_target_pairs={{0,1},{1,0},{2,3},{3,2},{4,5},{5,4},{6,7},{7,6},{8,9},{9,8},{10,11... | collective-permute-start | bytes 2359304 | tf_op jit(solution)/shard_map/other_rows/ppermute | solution.py:167
  40.9 5.1 %all-to-all-start.1 = ((bf16[32,8,1536]{2,1,0:T(8,128)(2,1)}), bf16[32,8,1536]{2,1,0:T(8,128)(2,1)S(1)}, u32[]{:S(2)}, u32[]{:S(2)}) async-start(bf16[32,8,1536]{2,1,0:T(8,128)(2,1)} %bitcast.3), calls=%async_computation.1 | async-start | bytes 1572864 | tf_op jit(solution)/shard_map/screened/all_to_all | solution.py:153
  46.0 0.0 collective-permute-done
  46.0 0.1 select_bitcast_fusion.1
  46.1 0.1 pad_maximum_fusion
  46.3 22.9 %all-to-all-done.1 = bf16[32,8,1536]{2,1,0:T(8,128)(2,1)S(1)} async-done(((bf16[32,8,1536]{2,1,0:T(8,128)(2,1)}), bf16[32,8,1536]{2,1,0:T(8,128)(2,1)S(1)}, u32[]{:S(2)}, u32[]{:S(2)}) %all-to-all-start.1) | async-done | bytes 786464 | tf_op jit(solution)/shard_map/screened/all_to_all | solution.py:153
  69.2 0.6 fusion
  69.8 17.7 %all_to_all.20 = bf16[32,8,512]{2,1,0:T(8,128)(2,1)S(1)} all-to-all(bf16[32,8,512]{2,1,0:T(8,128)(2,1)S(1)} %fusion), channel_id=1, replica_groups={{0,2,4,6,8,10,12,14,16,18,20,22,24,26,28,30,32,34,36,38,40,42,44,46,48,..., dimensions={0} | all-to-all | bytes 524288 | tf_op jit(solution)/shard_map/over_plane/all_to_all | solution.py:153
  87.6 26.4 %all_to_all.21 = f32[12,8,512]{2,1,0:T(8,128)S(1)} all-to-all(f32[12,8,512]{2,1,0:T(8,128)S(1)} %broadcast_in_dim.2), channel_id=1, replica_groups=mesh['occ'=12,'tens'=64] {'occ'}, dimensions={0} | all-to-all | bytes 393216 | tf_op jit(solution)/shard_map/over_batches/all_to_all | solution.py:181
  113.9 0.6 broadcast_multiply_fusion
  (3 shorter events, 0.1 us)
Async XLA Ops:
  0.0 3.7 %copy-start = (bf16[8,768,768]{2,1,0:T(8,128)(2,1)S(1)}, bf16[8,768,768]{2,1,0:T(8,128)(2,1)}, u32[]{:S(2)}) copy-start(bf16[8,768,768]{2,1,0:T(8,128)(2,1)} %tensor_ref.3) | copy-start | bytes 28311556
  3.7 0.7 copy-start.4
  5.9 10.1 %copy-start.2 = (bf16[768,768]{1,0:T(8,128)(2,1)S(1)}, bf16[768,768]{1,0:T(8,128)(2,1)}, u32[]{:S(2)}) copy-start(bf16[768,768]{1,0:T(8,128)(2,1)} %virt_ref.1) | copy-start | bytes 3538948
  5.9 10.1 %copy-start.3 = (bf16[64,768]{1,0:T(8,128)(2,1)S(1)}, bf16[64,768]{1,0:T(8,128)(2,1)}, u32[]{:S(2)}) copy-start(bf16[64,768]{1,0:T(8,128)(2,1)} %occ_ref.1) | copy-start | bytes 294916
  5.9 10.1 %copy-start.5 = (s32[12,12]{1,0:T(8,128)S(1)}, s32[12,12]{1,0:T(8,128)}, u32[]{:S(2)}) copy-start(s32[12,12]{1,0:T(8,128)} %tmask_ref.1) | copy-start | bytes 1732
  5.9 10.1 %copy-start.6 = (s32[12,12]{1,0:T(8,128)S(1)}, s32[12,12]{1,0:T(8,128)}, u32[]{:S(2)}) copy-start(s32[12,12]{1,0:T(8,128)} %omask_ref.1) | copy-start | bytes 1732
  5.9 10.2 %copy-start.7 = (s32[12,12]{1,0:T(8,128)S(1)}, s32[12,12]{1,0:T(8,128)}, u32[]{:S(2)}) copy-start(s32[12,12]{1,0:T(8,128)} %vmask_ref.1) | copy-start | bytes 1732
  6.0 33.0 %all-to-all-start = ((bf16[32,8,1536]{2,1,0:T(8,128)(2,1)}), bf16[32,8,1536]{2,1,0:T(8,128)(2,1)S(1)}, u32[]{:S(2)}, u32[]{:S(2)}) async-start(bf16[32,8,1536]{2,1,0:T(8,128)(2,1)} %bitcast.1), calls=%async_computation | async-start | bytes 1572864 | tf_op jit(solution)/shard_map/rows/all_to_all | solution.py:153
  16.1 3.7 %copy-start.1 = (bf16[8,768,768]{2,1,0:T(8,128)(2,1)S(1)}, bf16[8,768,768]{2,1,0:T(8,128)(2,1)}, u32[]{:S(2)}) copy-start(bf16[8,768,768]{2,1,0:T(8,128)(2,1)} %tensor_ref.3) | copy-start | bytes 28311556
  39.0 7.0 %collective-permute-start = (bf16[256,1536]{1,0:T(8,128)(2,1)S(1)}, bf16[256,1536]{1,0:T(8,128)(2,1)S(1)}, u32[]{:S(2)}, u32[]{:S(2)}) collective-permute-start(bf16[256,1536]{1,0:T(8,128)(2,1)S(1)} %bitcast.15), channel_id=1, source_target_pairs={{0,1},{1,0},{2,3},{3,2},{4,5},{5,4},{6,7},{7,6},{8,9},{9,8},{10,11... | collective-permute-start | bytes 2359304 | tf_op jit(solution)/shard_map/other_rows/ppermute | solution.py:167
  40.9 28.3 %all-to-all-start.1 = ((bf16[32,8,1536]{2,1,0:T(8,128)(2,1)}), bf16[32,8,1536]{2,1,0:T(8,128)(2,1)S(1)}, u32[]{:S(2)}, u32[]{:S(2)}) async-start(bf16[32,8,1536]{2,1,0:T(8,128)(2,1)} %bitcast.3), calls=%async_computation.1 | async-start | bytes 1572864 | tf_op jit(solution)/shard_map/screened/all_to_all | solution.py:153

commit v3 on v2

--- a/solution.py
+++ b/solution.py
@@ -96,7 +96,7 @@
             out_specs=pl.BlockSpec(shape, lambda s, batch: (0, 0)),
             scratch_shapes=[pltpu.VMEM((shape[1] // LANES, shape[0], LANES), F32)],
         ),
-        compiler_params=pltpu.CompilerParams(vmem_limit_bytes=16 * 2**20),
+        compiler_params=pltpu.CompilerParams(vmem_limit_bytes=56 * 2**20),
         name="row_messages",
     )(batch, tensor, tensor_mask)
 
@@ -130,7 +130,7 @@
                 pltpu.VMEM((shape[1] // LANES, shape[0], LANES), F32),
             ],
         ),
-        compiler_params=pltpu.CompilerParams(vmem_limit_bytes=28 * 2**20),
+        compiler_params=pltpu.CompilerParams(vmem_limit_bytes=56 * 2**20),
         cost_estimate=pl.CostEstimate(
             flops=4 * work, bytes_accessed=2 * tensor.size + 4 * virt_green.size, transcendentals=0
         ),
@@ -167,6 +167,7 @@
         sibling_rows = lax.ppermute(moved_rows, "tens", other_core)
     with jax.named_scope("screened"):
         moved_screened = regroup(screened)
+    moved_screened, sibling_rows = lax.optimization_barrier((moved_screened, sibling_rows))
     own = moved_rows.reshape(chips, 1, local_ri, -1)
     other = sibling_rows.reshape(chips, 1, local_ri, -1)
     first = jnp.where(core == 0, own, other)

time: 115 us -> 108 us (0.939)
  the two profiles are of different devices: /device:TPU:64 before, /device:TPU:8 now
where the time goes in v3:
time: 108 us; the launch traced here: 107 us
  blocking collectives  45.4 us (42%)
  waiting for transfers between devices  25.6 us (24%)
  starting transfers between devices  20.6 us (19%)
  Pallas kernels  13.8 us (13%)
    all_to_all x1, blocking collectives, body(): batch_shares = lax.all_to_all(copies, 'occ', 0, 0, tiled=True)  29.1 us
    all_to_all x2, waiting for transfers between devices, over_plane(): lax.all_to_all(values, 'tens', 0, 0, axis_index_groups=same_core, tiled=T...  23.4 us
    all_to_all x2, starting transfers between devices, over_plane(): lax.all_to_all(values, 'tens', 0, 0, axis_index_groups=same_core, tiled=T...  18.7 us
    all_to_all x1, blocking collectives, over_plane(): lax.all_to_all(values, 'tens', 0, 0, axis_index_groups=same_core, tiled=T...  16.2 us
    pallas_call x1, Pallas kernels, screened_messages(): pl.pallas_call(screened_kernel, out_shape=jax.ShapeDtypeStruct(shape, BF1...  11.1 us
    pallas_call x1, Pallas kernels, row_messages(): pl.pallas_call(rows_kernel, out_shape=jax.ShapeDtypeStruct(shape, BF16),...  2.71 us
    ppermute x1, waiting for transfers between devices, body(): sibling_rows = lax.ppermute(moved_rows, 'tens', other_core)  2.24 us
  transfers between devices with their start and end apart: 3, of which 3 were waited for; matrix products, arithmetic and copies ran while one was open for 0% of the time, Pallas kernels for 10%

profile of v3, /device:TPU:8, one launch (start us, length us, event | category | flops | bytes accessed | tf_op | source)
XLA Modules:
  0.0 107.0 jit_solution(7820347267561644296)
XLA Ops:
  0.0 2.7 %row_messages.1 = bf16[256,1536]{1,0:T(8,128)(2,1)} custom-call(s32[1]{0:T(128)} %bitcast.batch_ref, bf16[8,768,768]{2,1,0:T(8,128)(2,1)} %tensor_ref.3, s32[12,12]{1,0:T(8,128)} %tmask_ref.1), custom_call_target="tpu_custom_call" | custom-call | tf_op jit(solution)/shard_map/row_messages/pallas_call | solution.py:86
  2.7 13.0 %all-to-all-start = ((bf16[32,8,1536]{2,1,0:T(8,128)(2,1)}), bf16[32,8,1536]{2,1,0:T(8,128)(2,1)S(1)}, u32[]{:S(2)}, u32[]{:S(2)}) async-start(bf16[32,8,1536]{2,1,0:T(8,128)(2,1)} %bitcast.15), calls=%async_computation | async-start | bytes 1572864 | tf_op jit(solution)/shard_map/rows/all_to_all | solution.py:153
  15.8 11.1 %screened_messages.1 = bf16[256,1536]{1,0:T(8,128)(2,1)} custom-call(s32[1]{0:T(128)} %bitcast.batch_ref, bf16[8,768,768]{2,1,0:T(8,128)(2,1)} %tensor_ref.3, bf16[64,768]{1,0:T(8,128)(2,1)} %occ_ref.1, bf16[768,768]{1,0:T(8,128)(2,1)} %virt_ref.1, s32[12,12]{1,0:T(8,128)} %tmask_ref.1, s32[12,12]{1,0:T(8,128)} %omask_ref.1, s32[12,12]{1,0:T(8,128)} %vmask_ref.1), custom_call_target="tpu_custom_call" | custom-call | flops 1207959552 | bytes 11796480 | tf_op jit(solution)/shard_map/screened_messages/pallas_call | solution.py:111
  26.8 8.4 %all-to-all-done = bf16[32,8,1536]{2,1,0:T(8,128)(2,1)S(1)} async-done(((bf16[32,8,1536]{2,1,0:T(8,128)(2,1)}), bf16[32,8,1536]{2,1,0:T(8,128)(2,1)S(1)}, u32[]{:S(2)}, u32[]{:S(2)}) %all-to-all-start) | async-done | bytes 786464 | tf_op jit(solution)/shard_map/rows/all_to_all | solution.py:153
  35.3 5.6 %all-to-all-start.1 = ((bf16[32,8,1536]{2,1,0:T(8,128)(2,1)}), bf16[32,8,1536]{2,1,0:T(8,128)(2,1)S(1)}, u32[]{:S(2)}, u32[]{:S(2)}) async-start(bf16[32,8,1536]{2,1,0:T(8,128)(2,1)} %bitcast.14), calls=%async_computation.1 | async-start | bytes 1572864 | tf_op jit(solution)/shard_map/screened/all_to_all | solution.py:153
  40.9 1.9 %collective-permute-start = (bf16[256,1536]{1,0:T(8,128)(2,1)S(1)}, bf16[256,1536]{1,0:T(8,128)(2,1)S(1)}, u32[]{:S(2)}, u32[]{:S(2)}) collective-permute-start(bf16[256,1536]{1,0:T(8,128)(2,1)S(1)} %bitcast.16), channel_id=1, source_target_pairs={{0,1},{1,0},{2,3},{3,2},{4,5},{5,4},{6,7},{7,6},{8,9},{9,8},{10,11... | collective-permute-start | bytes 2359304 | tf_op jit(solution)/shard_map/other_rows/ppermute | solution.py:167
  42.8 2.2 %collective-permute-done = bf16[256,1536]{1,0:T(8,128)(2,1)S(1)} collective-permute-done((bf16[256,1536]{1,0:T(8,128)(2,1)S(1)}, bf16[256,1536]{1,0:T(8,128)(2,1)S(1)}, u32[]{:S(2)}, u32[]{:S(2)}) %collective-permute-start) | collective-permute-done | bytes 786464 | tf_op jit(solution)/shard_map/other_rows/ppermute | solution.py:167
  45.1 15.0 %all-to-all-done.1 = bf16[32,8,1536]{2,1,0:T(8,128)(2,1)S(1)} async-done(((bf16[32,8,1536]{2,1,0:T(8,128)(2,1)}), bf16[32,8,1536]{2,1,0:T(8,128)(2,1)S(1)}, u32[]{:S(2)}, u32[]{:S(2)}) %all-to-all-start.1) | async-done | bytes 786464 | tf_op jit(solution)/shard_map/screened/all_to_all | solution.py:153
  60.1 0.1 select_bitcast_fusion.1
  60.2 0.1 pad_maximum_fusion
  60.3 0.6 fusion
  60.9 16.2 %all_to_all.20 = bf16[32,8,512]{2,1,0:T(8,128)(2,1)S(1)} all-to-all(bf16[32,8,512]{2,1,0:T(8,128)(2,1)S(1)} %fusion), channel_id=1, replica_groups={{0,2,4,6,8,10,12,14,16,18,20,22,24,26,28,30,32,34,36,38,40,42,44,46,48,..., dimensions={0} | all-to-all | bytes 524288 | tf_op jit(solution)/shard_map/over_plane/all_to_all | solution.py:153
  77.2 29.1 %all_to_all.21 = f32[12,8,512]{2,1,0:T(8,128)S(1)} all-to-all(f32[12,8,512]{2,1,0:T(8,128)S(1)} %broadcast_in_dim.2), channel_id=1, replica_groups=mesh['occ'=12,'tens'=64] {'occ'}, dimensions={0} | all-to-all | bytes 393216 | tf_op jit(solution)/shard_map/over_batches/all_to_all | solution.py:182
  106.4 0.6 broadcast_multiply_fusion
  (3 shorter events, 0.1 us)
Async XLA Ops:
  2.7 32.5 %all-to-all-start = ((bf16[32,8,1536]{2,1,0:T(8,128)(2,1)}), bf16[32,8,1536]{2,1,0:T(8,128)(2,1)S(1)}, u32[]{:S(2)}, u32[]{:S(2)}) async-start(bf16[32,8,1536]{2,1,0:T(8,128)(2,1)} %bitcast.15), calls=%async_computation | async-start | bytes 1572864 | tf_op jit(solution)/shard_map/rows/all_to_all | solution.py:153
  35.3 24.8 %all-to-all-start.1 = ((bf16[32,8,1536]{2,1,0:T(8,128)(2,1)}), bf16[32,8,1536]{2,1,0:T(8,128)(2,1)S(1)}, u32[]{:S(2)}, u32[]{:S(2)}) async-start(bf16[32,8,1536]{2,1,0:T(8,128)(2,1)} %bitcast.14), calls=%async_computation.1 | async-start | bytes 1572864 | tf_op jit(solution)/shard_map/screened/all_to_all | solution.py:153
  40.9 4.2 %collective-permute-start = (bf16[256,1536]{1,0:T(8,128)(2,1)S(1)}, bf16[256,1536]{1,0:T(8,128)(2,1)S(1)}, u32[]{:S(2)}, u32[]{:S(2)}) collective-permute-start(bf16[256,1536]{1,0:T(8,128)(2,1)S(1)} %bitcast.16), channel_id=1, source_target_pairs={{0,1},{1,0},{2,3},{3,2},{4,5},{5,4},{6,7},{7,6},{8,9},{9,8},{10,11... | collective-permute-start | bytes 2359304 | tf_op jit(solution)/shard_map/other_rows/ppermute | solution.py:167

commit v4 on v3

v4 whole, which is shorter than its diff:
```python
import functools

import jax
import jax.numpy as jnp
from jax import lax
from jax.experimental import pallas as pl
from jax.experimental.pallas import tpu as pltpu
from jax.sharding import PartitionSpec as P

BLOCK = 64
LANES = 128
BF16 = jnp.bfloat16
F32 = jnp.float32


def block_of(size, blocks):
    position = lax.broadcasted_iota(jnp.int32, (size, blocks), 0)
    start = lax.broadcasted_iota(jnp.int32, (size, blocks), 1) * BLOCK
    return ((position >= start) & (position < start + BLOCK)).astype(BF16)


def dot(a, b):
    return jnp.dot(a, b, preferred_element_type=F32)


def dot_t(a, b):
    return lax.dot_general(a, b, (((1,), (1,)), ((), ())), preferred_element_type=F32)


def as_bf16(pattern):
    return pattern.astype(F32).astype(BF16)


def spread(pattern, rows, columns):
    across = dot_t(as_bf16(pattern), block_of(columns, pattern.shape[1])).astype(BF16)
    return dot(block_of(rows, pattern.shape[0]), across).astype(BF16)


def kept_blocks(batch, mask_ref, kept):
    count = jnp.int32(0)
    for block in range(mask_ref.shape[1]):
        kept[count] = block
        count = count + mask_ref[batch, block]
    return count


def placement(rows, local_ri):
    shift = local_ri.bit_length() - 1
    to = lax.broadcasted_iota(jnp.int32, (rows, rows), 0)
    source = lax.broadcasted_iota(jnp.int32, (rows, rows), 1)
    wanted = (to & (local_ri - 1)) * (rows // local_ri) + (to >> shift)
    return (wanted == source).astype(F32).astype(BF16)


def gather_blocks(read, kept, count, out_ref, first, last):
    rows = out_ref.shape[0]
    side = lax.broadcasted_iota(jnp.int32, (rows, LANES), 1) // BLOCK
    for slot in range(first, last):
        columns = slice(slot * LANES, (slot + 1) * LANES)

        @pl.when(slot < count)
        def _():
            block = kept[slot]
            odd = block % 2
            direct = read(odd, block // 2)
            rolled = pltpu.roll(read(1 - odd, block // 2), BLOCK, 1)
            out_ref[:, columns] = jnp.where(side == odd, direct, rolled).astype(BF16)

        @pl.when(slot >= count)
        def _():
            out_ref[:, columns] = jnp.zeros((rows, LANES), BF16)


def rows_kernel(sizes, mask_hbm, tensor_ref, *refs):
    outs = refs[: len(sizes)]
    choice_hbm, mask_ref, choice_ref, slab, ordered, messages, kept, arrived = refs[len(sizes) :]
    local_ri, rows, columns = slab.shape
    chips = rows // 2
    batch = lax.axis_index("occ")
    start = pl.multiple_of(batch * rows, rows)
    mask_copy = pltpu.make_async_copy(mask_hbm, mask_ref, arrived.at[0])
    mask_copy.start()
    copy = pltpu.make_async_copy(tensor_ref.at[:, pl.ds(start, rows), :], slab, arrived.at[1])
    copy.start()
    place = placement(local_ri * chips, local_ri)
    mask_copy.wait()
    fullest = jnp.int32(0)
    for row in range(mask_ref.shape[0]):
        total = jnp.int32(0)
        for block in range(mask_ref.shape[1]):
            total = total + mask_ref[row, block]
        fullest = jnp.maximum(fullest, total)
    choice = jnp.clip(fullest - sizes[0], 0, len(sizes) - 1)
    choice_ref[0] = choice
    choice_copy = pltpu.make_async_copy(choice_ref, choice_hbm, arrived.at[2])
    choice_copy.start()
    count = kept_blocks(batch, mask_ref, kept)
    copy.wait()
    for half in range(2):
        values = slab[:, half * chips : (half + 1) * chips, :].reshape(local_ri * chips, columns)
        values = dot(place, values)
        for tile in range(columns // LANES):
            ordered[half, tile] = values[:, tile * LANES : (tile + 1) * LANES]

    def send(index, first, last, semaphore):
        columns = slice(first * LANES, last * LANES)
        return pltpu.make_async_copy(
            messages.at[:, columns], outs[index].at[:, columns], arrived.at[semaphore]
        )

    read = lambda half, tile: ordered[half, tile]
    gather_blocks(read, kept, count, messages, 0, sizes[0])
    for index in range(len(sizes)):

        @pl.when(choice == index)
        def _():
            send(index, 0, sizes[0], 3).start()

    gather_blocks(read, kept, count, messages, sizes[0], sizes[-1])
    for index, slots in enumerate(sizes):

        @pl.when(choice == index)
        def _():
            if slots > sizes[0]:
                rest = send(index, sizes[0], slots, 4)
                rest.start()
                rest.wait()
            send(index, 0, sizes[0], 3).wait()

    choice_copy.wait()


def screened_kernel(
    batch_ref, mask_ref, tensor_ref, occ_ref, virt_ref, tmask_ref, omask_ref, vmask_ref, out_ref,
    keep, occ_part, virt_part, occ_half, staged, kept,
):
    index = pl.program_id(0)
    local_ri = occ_half.shape[1]
    ao_count = virt_ref.shape[0]
    chips = occ_ref.shape[0] // 2

    @pl.when(index == 0)
    def _():
        keep[...] = spread(tmask_ref[...], ao_count, ao_count)
        virt_part[...] = virt_ref[...] * spread(vmask_ref[...], ao_count, ao_count)
        pattern = as_bf16(omask_ref[pl.ds(batch_ref[0], 1), :])
        row_keep = dot_t(pattern, block_of(ao_count, pattern.shape[1])).astype(BF16)
        occ_part[...] = occ_ref[...] * row_keep

    product = dot(occ_part[...], tensor_ref[0] * keep[...]).astype(BF16)
    occ_half[0, index] = product[:chips]
    occ_half[1, index] = product[chips:]

    @pl.when(index == local_ri - 1)
    def _():
        count = kept_blocks(batch_ref[0], mask_ref, kept)
        place = placement(local_ri * chips, local_ri)
        for half in range(2):
            values = dot(occ_half[half].reshape(local_ri * chips, ao_count), virt_part[...])
            ordered = dot(place, values.astype(BF16))
            for tile in range(ao_count // LANES):
                staged[half, tile] = ordered[:, tile * LANES : (tile + 1) * LANES]
        slots = out_ref.shape[1] // LANES
        gather_blocks(lambda half, tile: staged[half, tile], kept, count, out_ref, 0, slots)


def row_messages(sizes, tensor_mask, tensor, rows):
    local_ri, _, columns = tensor.shape
    count = rows // 2 * local_ri
    shapes = [jax.ShapeDtypeStruct((count, slots * LANES), BF16) for slots in sizes]
    anywhere = pl.BlockSpec(memory_space=pl.ANY)
    *messages, choice = pl.pallas_call(
        functools.partial(rows_kernel, sizes),
        out_shape=(*shapes, jax.ShapeDtypeStruct((1,), jnp.int32)),
        in_specs=[anywhere, anywhere],
        out_specs=(anywhere,) * (len(sizes) + 1),
        scratch_shapes=[
            pltpu.SMEM(tensor_mask.shape, jnp.int32),
            pltpu.SMEM((1,), jnp.int32),
            pltpu.VMEM((local_ri, rows, columns), BF16),
            pltpu.VMEM((2, columns // LANES, count, LANES), F32),
            pltpu.VMEM((count, 2 * columns), BF16),
            pltpu.SMEM((tensor_mask.shape[1] + 1,), jnp.int32),
            pltpu.SemaphoreType.DMA((5,)),
        ],
        compiler_params=pltpu.CompilerParams(vmem_limit_bytes=56 * 2**20),
        name="row_messages",
    )(tensor_mask, tensor)
    return messages, choice[0]


def screened_messages(
    slots, batch, tensor, occ_green, virt_green, tensor_mask, occ_mask, virt_mask
):
    local_ri, ao_count, _ = tensor.shape
    rows = occ_green.shape[0]
    chips = rows // 2
    whole = lambda s, batch, mask: (0, 0)
    pattern = pl.BlockSpec(tensor_mask.shape, whole)
    work = local_ri * rows * ao_count * ao_count
    return pl.pallas_call(
        screened_kernel,
        out_shape=jax.ShapeDtypeStruct((chips * local_ri, slots * LANES), BF16),
        grid_spec=pltpu.PrefetchScalarGridSpec(
            num_scalar_prefetch=2,
            grid=(local_ri,),
            in_specs=[
                pl.BlockSpec((1, ao_count, ao_count), lambda s, batch, mask: (s, 0, 0)),
                pl.BlockSpec(occ_green.shape, whole),
                pl.BlockSpec(virt_green.shape, whole),
                pattern,
                pattern,
                pattern,
            ],
            out_specs=pl.BlockSpec((chips * local_ri, slots * LANES), whole),
            scratch_shapes=[
                pltpu.VMEM((ao_count, ao_count), BF16),
                pltpu.VMEM(occ_green.shape, BF16),
                pltpu.VMEM(virt_green.shape, BF16),
                pltpu.VMEM((2, local_ri, chips, ao_count), BF16),
                pltpu.VMEM((2, ao_count // LANES, chips * local_ri, LANES), F32),
                pltpu.SMEM((tensor_mask.shape[1] + 1,), jnp.int32),
            ],
        ),
        compiler_params=pltpu.CompilerParams(vmem_limit_bytes=56 * 2**20),
        cost_estimate=pl.CostEstimate(
            flops=4 * work, bytes_accessed=2 * tensor.size + 4 * virt_green.size, transcendentals=0
        ),
        name="screened_messages",
    )(batch, tensor_mask, tensor, occ_green, virt_green, tensor_mask, occ_mask, virt_mask)


def body(tensor, occ_green, virt_green, tensor_mask, occ_mask, virt_mask):
    rows_batch, ao_count = occ_green.shape
    local_ri = tensor.shape[0]
    batches = lax.axis_size("occ")
    cells = lax.axis_size("tens")
    chips = cells // 2
    same_core = [[2 * chip + core for chip in range(chips)] for core in range(2)]
    other_core = [(cell, cell ^ 1) for cell in range(cells)]
    batch = lax.axis_index("occ").astype(jnp.int32).reshape(1)
    core = lax.axis_index("tens") % 2

    def over_plane(values):
        return lax.all_to_all(values, "tens", 0, 0, axis_index_groups=same_core, tiled=True)

    def regroup(messages):
        moved = over_plane(messages.reshape(chips, local_ri, -1))
        return moved.reshape(chips * local_ri, -1)

    blocks = tensor_mask.shape[1]
    sizes = list(range(blocks // 2, blocks + 1))
    messages, choice = row_messages(sizes, tensor_mask, tensor, rows_batch)

    def partial_with(index):
        slots = sizes[index]

        def partial_value():
            with jax.named_scope("rows"):
                moved_rows = regroup(messages[index])
            screened = screened_messages(
                slots, batch, tensor, occ_green, virt_green, tensor_mask, occ_mask, virt_mask
            )
            moved_rows, screened = lax.optimization_barrier((moved_rows, screened))
            with jax.named_scope("other_rows"):
                sibling_rows = lax.ppermute(moved_rows, "tens", other_core)
            with jax.named_scope("screened"):
                moved_screened = regroup(screened)
            moved_screened, sibling_rows = lax.optimization_barrier((moved_screened, sibling_rows))
            own = moved_rows.reshape(chips, 1, local_ri, -1)
            other = sibling_rows.reshape(chips, 1, local_ri, -1)
            first = jnp.where(core == 0, own, other)
            second = jnp.where(core == 0, other, own)
            all_rows = jnp.concatenate([first, second], axis=1)
            all_rows = all_rows.reshape(2 * chips * local_ri, -1)
            return dot_t(moved_screened, all_rows).astype(BF16)

        return partial_value

    branches = [partial_with(index) for index in range(len(sizes))]
    partial_value = lax.switch(choice, branches)
    with jax.named_scope("over_plane"):
        shares = over_plane(partial_value.reshape(chips, local_ri, -1))
    batch_share = jnp.sum(shares.astype(F32), axis=0)
    copies = jnp.broadcast_to(batch_share[None], (batches,) + batch_share.shape)
    with jax.named_scope("over_batches"):
        batch_shares = lax.all_to_all(copies, "occ", 0, 0, tiled=True)
    return jnp.sum(batch_shares, axis=0) * (-1.0 / ao_count)


def solution(mesh):
    in_specs = (P("tens", None, None), P("occ", None), P(), P(), P(), P())
    out_specs = P("tens", None)
    return jax.shard_map(body, mesh=mesh, in_specs=in_specs, out_specs=out_specs, check_vma=False)
```

time: 108 us -> 108 us (level)
  waiting for transfers between devices: 25.6 us -> 22.5 us
  Pallas kernels: 13.8 us -> 15 us
  other arithmetic: 0.92 us -> 2.08 us
    all_to_all x2, waiting for transfers between devices: 23.4 us -> 20.3 us  [over_plane(): lax.all_to_all(values, 'tens', 0, 0, axis_index_groups=same_core, tiled=T...]
    pallas_call x2, Pallas kernels: 13.8 us -> 15 us  [the longest x1 11.8 us: screened_messages(): pl.pallas_call(screened_kernel, out_shape=jax.ShapeDtypeStruct((chips * l...]
    select_n x1, other arithmetic: 0.11 us -> 1.24 us  [partial_value(): first = jnp.where(core == 0, own, other)]
  transfers between devices with their start and end apart: 3 -> 3, of which waited for: 3 -> 3; matrix products, arithmetic and copies ran while one was open for 0% -> 0% of each run, Pallas kernels for 10% -> 11%
where the time goes in v4:
time: 108 us
  blocking collectives  45.3 us (42%)
  waiting for transfers between devices  22.5 us (21%)
  starting transfers between devices  20.5 us (19%)
  Pallas kernels  15 us (14%)
  other arithmetic  2.08 us (2%)
    all_to_all x1, blocking collectives, body(): batch_shares = lax.all_to_all(copies, 'occ', 0, 0, tiled=True)  29.2 us
    all_to_all x2, waiting for transfers between devices, over_plane(): lax.all_to_all(values, 'tens', 0, 0, axis_index_groups=same_core, tiled=T...  20.3 us
    all_to_all x2, starting transfers between devices, over_plane(): lax.all_to_all(values, 'tens', 0, 0, axis_index_groups=same_core, tiled=T...  18.6 us
    all_to_all x1, blocking collectives, over_plane(): lax.all_to_all(values, 'tens', 0, 0, axis_index_groups=same_core, tiled=T...  16.1 us
    pallas_call x1, Pallas kernels, screened_messages(): pl.pallas_call(screened_kernel, out_shape=jax.ShapeDtypeStruct((chips * l...  11.8 us
    pallas_call x1, Pallas kernels, row_messages(): pl.pallas_call(functools.partial(rows_kernel, sizes), out_shape=(*shapes,...  3.24 us
  transfers between devices with their start and end apart: 3, of which 3 were waited for; matrix products, arithmetic and copies ran while one was open for 0% of the time, Pallas kernels for 11%

profile of v4, /device:TPU:8, one launch (start us, length us, event | category | flops | bytes accessed | tf_op | source)
XLA Modules:
  0.0 107.8 jit_solution(15266985498339014677)
XLA Ops:
  0.0 0.0 copy-start
  0.0 0.0 copy-start.1
  0.0 0.0 copy-start.2
  0.0 0.0 copy-start.5
  0.0 0.0 copy-start.6
  0.0 3.2 %row_messages.1 = (bf16[256,768]{1,0:T(8,128)(2,1)}, bf16[256,896]{1,0:T(8,128)(2,1)}, bf16[256,1024]{1,0:T(8,128)(2,1)}, bf16[256,1152]{1,0:T(8,128)(2,1)}, bf1...) custom-call(s32[12,12]{1,0:T(8,128)} %mask_hbm.1, ...), custom_call_target="tpu_custom_call" | custom-call | tf_op jit(solution)/shard_map/row_messages/pallas_call | solution.py:172
  3.9 0.0 copy-done
  3.9 0.0 copy-done.1
  4.0 0.0 copy-done.2
  4.0 0.0 copy-done.5
  4.0 0.0 copy-done.6
  4.0 57.7 %conditional.2 = (bf16[256,512]{1,0:T(8,128)(2,1)S(1)}) conditional(s32[]{:T(128)} %bitcast.49, (bf16[256,768]{1,0:T(8,128)(2,1)}, s32[1]{0:T(128)}, s32[12,12]{1,0:T(8,128)S(1)}, bf16[8,768,768]{2,1,0:T(8,128)(2,1)}, bf16[64,768]{1,0:T(8,128)(2,1)S(1)}, /*index=5*/bf16[768,768]{1,0:T(8,128)(2,1)S(1)}, ...), branch_computations={%region_0.1_spmd, %region_1.2_spmd, %region_2.3_spmd, %region_3.4_... | conditional | flops 1612185600 | bytes 31719572
  4.2 13.1 %all-to-all-start.10 = ((bf16[32,8,1408]{2,1,0:T(8,128)(2,1)}), bf16[32,8,1408]{2,1,0:T(8,128)(2,1)S(1)}, u32[]{:S(2)}, u32[]{:S(2)}) async-start(bf16[32,8,1408]{2,1,0:T(8,128)(2,1)} %bitcast.35), calls=%async_computation.10 | async-start | bytes 1441792 | tf_op jit(solution)/shard_map/cond/branch_5_fun/rows/all_to_all | solution.py:245
  17.3 11.8 %screened_messages.12 = bf16[256,1408]{1,0:T(8,128)(2,1)} custom-call(s32[1]{0:T(128)} %get-tuple-element.207.batch_ref, s32[12,12]{1,0:T(8,128)S(1)} %get-tuple-element.208.mask_ref.tmask_ref, bf16[8,768,768]{2,1,0:T(8,128)(2,1)} %get-tuple-element.209.tensor_ref, bf16[64,768]{1,0:T(8,128)(2,1)S(1)} %get-tuple-element.210.occ_ref, ...), custom_call_target="tpu_custom_call" | custom-call | flops 1207959552 | bytes 11796480 | tf_op jit(solution)/shard_map/cond/branch_5_fun/screened_messages/pallas_call | solution.py:201
  29.1 6.4 %all-to-all-done.10 = bf16[32,8,1408]{2,1,0:T(8,128)(2,1)S(1)} async-done(((bf16[32,8,1408]{2,1,0:T(8,128)(2,1)}), bf16[32,8,1408]{2,1,0:T(8,128)(2,1)S(1)}, u32[]{:S(2)}, u32[]{:S(2)}) %all-to-all-start.10) | async-done | bytes 720928 | tf_op jit(solution)/shard_map/cond/branch_5_fun/rows/all_to_all | solution.py:245
  35.5 5.5 %all-to-all-start.11 = ((bf16[32,8,1408]{2,1,0:T(8,128)(2,1)}), bf16[32,8,1408]{2,1,0:T(8,128)(2,1)S(1)}, u32[]{:S(2)}, u32[]{:S(2)}) async-start(bf16[32,8,1408]{2,1,0:T(8,128)(2,1)} %bitcast.90), calls=%async_computation.11 | async-start | bytes 1441792 | tf_op jit(solution)/shard_map/cond/branch_5_fun/screened/all_to_all | solution.py:245
  41.0 1.9 %collective-permute-start.5 = (bf16[256,1408]{1,0:T(8,128)(2,1)S(1)}, bf16[256,1408]{1,0:T(8,128)(2,1)S(1)}, u32[]{:S(2)}, u32[]{:S(2)}) collective-permute-start(bf16[256,1408]{1,0:T(8,128)(2,1)S(1)} %bitcast.88), channel_id=1, source_target_pairs={{0,1},{1,0},{2,3},{3,2},{4,5},{5,4},{6,7},{7,6},{8,9},{9,8},{10,11... | collective-permute-start | bytes 2162696 | tf_op jit(solution)/shard_map/cond/branch_5_fun/other_rows/ppermute | solution.py:266
  43.0 2.2 %collective-permute-done.5 = bf16[256,1408]{1,0:T(8,128)(2,1)S(1)} collective-permute-done((bf16[256,1408]{1,0:T(8,128)(2,1)S(1)}, bf16[256,1408]{1,0:T(8,128)(2,1)S(1)}, u32[]{:S(2)}, u32[]{:S(2)}) %collective-permute-start.5) | collective-permute-done | bytes 720928 | tf_op jit(solution)/shard_map/cond/branch_5_fun/other_rows/ppermute | solution.py:266
  45.1 0.0 copy-start.4
  45.1 13.9 %all-to-all-done.11 = bf16[32,8,1408]{2,1,0:T(8,128)(2,1)S(1)} async-done(((bf16[32,8,1408]{2,1,0:T(8,128)(2,1)}), bf16[32,8,1408]{2,1,0:T(8,128)(2,1)S(1)}, u32[]{:S(2)}, u32[]{:S(2)}) %all-to-all-start.11) | async-done | bytes 720928 | tf_op jit(solution)/shard_map/cond/branch_5_fun/screened/all_to_all | solution.py:245
  59.1 0.0 copy-done.4
  59.1 1.2 %select_bitcast_fusion.11 = (bf16[32,1,8,1408]{3,2,1,0:T(8,128)(2,1)S(1)}, bf16[32,1,8,1408]{3,2,1,0:T(8,128)(2,1)S(1)}) fusion(bf16[256,1408]{1,0:T(8,128)(2,1)S(1)} %bitcast.89, bf16[256,1408]{1,0:T(8,128)(2,1)} %copy-done.4, pred[]{:T(512)S(6)} %eq.26), kind=kLoop, calls=%fused_computation.17 | loop fusion | flops 720896 | bytes 2883585 | tf_op jit(solution)/shard_map/cond/branch_5_fun/jit(_where)/select_n | solution.py:272
  60.3 0.2 pad_maximum_fusion.5
  60.5 0.6 fusion.5
  61.7 16.1 %all_to_all.66 = bf16[32,8,512]{2,1,0:T(8,128)(2,1)S(1)} all-to-all(bf16[32,8,512]{2,1,0:T(8,128)(2,1)S(1)} %bitcast.113), channel_id=1, replica_groups={{0,2,4,6,8,10,12,14,16,18,20,22,24,26,28,30,32,34,36,38,40,42,44,46,48,..., dimensions={0} | all-to-all | bytes 524288 | tf_op jit(solution)/shard_map/over_plane/all_to_all | solution.py:245
  77.9 29.2 %all_to_all.67 = f32[12,8,512]{2,1,0:T(8,128)S(1)} all-to-all(f32[12,8,512]{2,1,0:T(8,128)S(1)} %broadcast_in_dim.2), channel_id=1, replica_groups=mesh['occ'=12,'tens'=64] {'occ'}, dimensions={0} | all-to-all | bytes 393216 | tf_op jit(solution)/shard_map/over_batches/all_to_all | solution.py:287
  107.1 0.6 broadcast_multiply_fusion
  (3 shorter events, 0.1 us)
Async XLA Ops:
  0.0 3.9 %copy-start = (bf16[768,768]{1,0:T(8,128)(2,1)S(1)}, bf16[768,768]{1,0:T(8,128)(2,1)}, u32[]{:S(2)}) copy-start(bf16[768,768]{1,0:T(8,128)(2,1)} %param.15) | copy-start | bytes 3538948
  0.0 3.9 %copy-start.1 = (bf16[64,768]{1,0:T(8,128)(2,1)S(1)}, bf16[64,768]{1,0:T(8,128)(2,1)}, u32[]{:S(2)}) copy-start(bf16[64,768]{1,0:T(8,128)(2,1)} %param.14) | copy-start | bytes 294916
  0.0 3.9 %copy-start.2 = (s32[12,12]{1,0:T(8,128)S(1)}, s32[12,12]{1,0:T(8,128)}, u32[]{:S(2)}) copy-start(s32[12,12]{1,0:T(8,128)} %mask_hbm.1) | copy-start | bytes 1732
  0.0 4.0 %copy-start.5 = (s32[12,12]{1,0:T(8,128)S(1)}, s32[12,12]{1,0:T(8,128)}, u32[]{:S(2)}) copy-start(s32[12,12]{1,0:T(8,128)} %param.17) | copy-start | bytes 1732
  0.0 4.0 %copy-start.6 = (s32[12,12]{1,0:T(8,128)S(1)}, s32[12,12]{1,0:T(8,128)}, u32[]{:S(2)}) copy-start(s32[12,12]{1,0:T(8,128)} %param.18) | copy-start | bytes 1732
  4.2 31.3 %all-to-all-start.10 = ((bf16[32,8,1408]{2,1,0:T(8,128)(2,1)}), bf16[32,8,1408]{2,1,0:T(8,128)(2,1)S(1)}, u32[]{:S(2)}, u32[]{:S(2)}) async-start(bf16[32,8,1408]{2,1,0:T(8,128)(2,1)} %bitcast.35), calls=%async_computation.10 | async-start | bytes 1441792 | tf_op jit(solution)/shard_map/cond/branch_5_fun/rows/all_to_all | solution.py:245
  35.5 23.5 %all-to-all-start.11 = ((bf16[32,8,1408]{2,1,0:T(8,128)(2,1)}), bf16[32,8,1408]{2,1,0:T(8,128)(2,1)S(1)}, u32[]{:S(2)}, u32[]{:S(2)}) async-start(bf16[32,8,1408]{2,1,0:T(8,128)(2,1)} %bitcast.90), calls=%async_computation.11 | async-start | bytes 1441792 | tf_op jit(solution)/shard_map/cond/branch_5_fun/screened/all_to_all | solution.py:245
  41.0 4.1 %collective-permute-start.5 = (bf16[256,1408]{1,0:T(8,128)(2,1)S(1)}, bf16[256,1408]{1,0:T(8,128)(2,1)S(1)}, u32[]{:S(2)}, u32[]{:S(2)}) collective-permute-start(bf16[256,1408]{1,0:T(8,128)(2,1)S(1)} %bitcast.88), channel_id=1, source_target_pairs={{0,1},{1,0},{2,3},{3,2},{4,5},{5,4},{6,7},{7,6},{8,9},{9,8},{10,11... | collective-permute-start | bytes 2162696 | tf_op jit(solution)/shard_map/cond/branch_5_fun/other_rows/ppermute | solution.py:266
  45.1 13.9 %copy-start.4 = (bf16[256,1408]{1,0:T(8,128)(2,1)}, bf16[256,1408]{1,0:T(8,128)(2,1)S(1)}, u32[]{:S(2)}) copy-start(bf16[256,1408]{1,0:T(8,128)(2,1)S(1)} %collective-permute-done.5) | copy-start | bytes 2162692 | tf_op jit(solution)/shard_map/conditional

commit v5 on v4

--- a/solution.py
+++ b/solution.py
@@ -84,17 +84,11 @@
     copy.start()
     place = placement(local_ri * chips, local_ri)
     mask_copy.wait()
-    fullest = jnp.int32(0)
-    for row in range(mask_ref.shape[0]):
-        total = jnp.int32(0)
-        for block in range(mask_ref.shape[1]):
-            total = total + mask_ref[row, block]
-        fullest = jnp.maximum(fullest, total)
-    choice = jnp.clip(fullest - sizes[0], 0, len(sizes) - 1)
+    count = kept_blocks(batch, mask_ref, kept)
+    choice = jnp.clip(count - sizes[0], 0, len(sizes) - 1)
     choice_ref[0] = choice
     choice_copy = pltpu.make_async_copy(choice_ref, choice_hbm, arrived.at[2])
     choice_copy.start()
-    count = kept_blocks(batch, mask_ref, kept)
     copy.wait()
     for half in range(2):
         values = slab[:, half * chips : (half + 1) * chips, :].reshape(local_ri * chips, columns)

time: 108 us -> 104 us (0.963)
  the two profiles are of different devices: /device:TPU:8 before, /device:TPU:64 now
where the time goes in v5:
time: 104 us; the launch traced here: 103 us
  blocking collectives  51.7 us (50%)
  starting transfers between devices  17.7 us (17%)
  waiting for transfers between devices  16.8 us (16%)
  Pallas kernels  14.4 us (14%)
    all_to_all x1, blocking collectives, body(): batch_shares = lax.all_to_all(copies, 'occ', 0, 0, tiled=True)  35.6 us
    all_to_all x1, blocking collectives, over_plane(): lax.all_to_all(values, 'tens', 0, 0, axis_index_groups=same_core, tiled=T...  16.2 us
    all_to_all x2, starting transfers between devices, over_plane(): lax.all_to_all(values, 'tens', 0, 0, axis_index_groups=same_core, tiled=T...  15.8 us
    all_to_all x2, waiting for transfers between devices, over_plane(): lax.all_to_all(values, 'tens', 0, 0, axis_index_groups=same_core, tiled=T...  15.1 us
    pallas_call x1, Pallas kernels, screened_messages(): pl.pallas_call(screened_kernel, out_shape=jax.ShapeDtypeStruct((chips * l...  11.4 us
    pallas_call x1, Pallas kernels, row_messages(): pl.pallas_call(functools.partial(rows_kernel, sizes), out_shape=(*shapes,...  2.93 us
  transfers between devices with their start and end apart: 3, of which 3 were waited for; matrix products, arithmetic and copies ran while one was open for 0% of the time, Pallas kernels for 11%

profile of v5, /device:TPU:64, one launch (start us, length us, event | category | flops | bytes accessed | tf_op | source)
XLA Modules:
  0.0 103.2 jit_solution(3527444859641970439)
XLA Ops:
  0.0 0.0 copy-start
  0.0 0.0 copy-start.1
  0.0 0.0 copy-start.2
  0.0 0.0 copy-start.5
  0.0 0.0 copy-start.6
  0.0 2.9 %row_messages.1 = (bf16[256,768]{1,0:T(8,128)(2,1)}, bf16[256,896]{1,0:T(8,128)(2,1)}, bf16[256,1024]{1,0:T(8,128)(2,1)}, bf16[256,1152]{1,0:T(8,128)(2,1)}, bf1...) custom-call(s32[12,12]{1,0:T(8,128)} %mask_hbm.1, ...), custom_call_target="tpu_custom_call" | custom-call | tf_op jit(solution)/shard_map/row_messages/pallas_call | solution.py:166
  3.6 0.0 copy-done
  3.6 0.0 copy-done.1
  3.6 0.0 copy-done.2
  3.6 0.0 copy-done.5
  3.7 0.0 copy-done.6
  3.7 47.1 %conditional.2 = (bf16[256,512]{1,0:T(8,128)(2,1)S(1)}) conditional(s32[]{:T(128)} %bitcast.49, (bf16[256,768]{1,0:T(8,128)(2,1)}, s32[1]{0:T(128)}, s32[12,12]{1,0:T(8,128)S(1)}, bf16[8,768,768]{2,1,0:T(8,128)(2,1)}, bf16[64,768]{1,0:T(8,128)(2,1)S(1)}, /*index=5*/bf16[768,768]{1,0:T(8,128)(2,1)S(1)}, ...), branch_computations={%region_0.1_spmd, %region_1.2_spmd, %region_2.3_spmd, %region_3.4_... | conditional | flops 1612185600 | bytes 31719572
  3.7 10.0 %all-to-all-start = ((bf16[32,8,768]{2,1,0:T(8,128)(2,1)}), bf16[32,8,768]{2,1,0:T(8,128)(2,1)S(1)}, u32[]{:S(2)}, u32[]{:S(2)}) async-start(bf16[32,8,768]{2,1,0:T(8,128)(2,1)} %bitcast), calls=%async_computation | async-start | bytes 786432 | tf_op jit(solution)/shard_map/cond/branch_0_fun/rows/all_to_all | solution.py:239
  13.7 11.4 %screened_messages.7 = bf16[256,768]{1,0:T(8,128)(2,1)} custom-call(s32[1]{0:T(128)} %get-tuple-element.140.batch_ref, s32[12,12]{1,0:T(8,128)S(1)} %get-tuple-element.142.mask_ref.tmask_ref, bf16[8,768,768]{2,1,0:T(8,128)(2,1)} %get-tuple-element.144.tensor_ref, bf16[64,768]{1,0:T(8,128)(2,1)S(1)} %get-tuple-element.145.occ_ref, ...), custom_call_target="tpu_custom_call" | custom-call | flops 1207959552 | bytes 11796480 | tf_op jit(solution)/shard_map/cond/branch_0_fun/screened_messages/pallas_call | solution.py:195
  25.1 3.9 %all-to-all-done = bf16[32,8,768]{2,1,0:T(8,128)(2,1)S(1)} async-done(((bf16[32,8,768]{2,1,0:T(8,128)(2,1)}), bf16[32,8,768]{2,1,0:T(8,128)(2,1)S(1)}, u32[]{:S(2)}, u32[]{:S(2)}) %all-to-all-start) | async-done | bytes 393248 | tf_op jit(solution)/shard_map/cond/branch_0_fun/rows/all_to_all | solution.py:239
  29.0 5.9 %all-to-all-start.1 = ((bf16[32,8,768]{2,1,0:T(8,128)(2,1)}), bf16[32,8,768]{2,1,0:T(8,128)(2,1)S(1)}, u32[]{:S(2)}, u32[]{:S(2)}) async-start(bf16[32,8,768]{2,1,0:T(8,128)(2,1)} %bitcast.105), calls=%async_computation.1 | async-start | bytes 786432 | tf_op jit(solution)/shard_map/cond/branch_0_fun/screened/all_to_all | solution.py:239
  34.9 1.9 %collective-permute-start = (bf16[256,768]{1,0:T(8,128)(2,1)S(1)}, bf16[256,768]{1,0:T(8,128)(2,1)S(1)}, u32[]{:S(2)}, u32[]{:S(2)}) collective-permute-start(bf16[256,768]{1,0:T(8,128)(2,1)S(1)} %bitcast.107), channel_id=1, source_target_pairs={{0,1},{1,0},{2,3},{3,2},{4,5},{5,4},{6,7},{7,6},{8,9},{9,8},{10,11... | collective-permute-start | bytes 1179656 | tf_op jit(solution)/shard_map/cond/branch_0_fun/other_rows/ppermute | solution.py:260
  36.8 1.7 %collective-permute-done = bf16[256,768]{1,0:T(8,128)(2,1)S(1)} collective-permute-done((bf16[256,768]{1,0:T(8,128)(2,1)S(1)}, bf16[256,768]{1,0:T(8,128)(2,1)S(1)}, u32[]{:S(2)}, u32[]{:S(2)}) %collective-permute-start) | collective-permute-done | bytes 393248 | tf_op jit(solution)/shard_map/cond/branch_0_fun/other_rows/ppermute | solution.py:260
  38.5 11.2 %all-to-all-done.1 = bf16[32,8,768]{2,1,0:T(8,128)(2,1)S(1)} async-done(((bf16[32,8,768]{2,1,0:T(8,128)(2,1)}), bf16[32,8,768]{2,1,0:T(8,128)(2,1)S(1)}, u32[]{:S(2)}, u32[]{:S(2)}) %all-to-all-start.1) | async-done | bytes 393248 | tf_op jit(solution)/shard_map/cond/branch_0_fun/screened/all_to_all | solution.py:239
  49.7 0.1 select_bitcast_fusion.1
  49.7 0.1 pad_maximum_fusion
  49.8 0.4 fusion
  50.8 16.2 %all_to_all.66 = bf16[32,8,512]{2,1,0:T(8,128)(2,1)S(1)} all-to-all(bf16[32,8,512]{2,1,0:T(8,128)(2,1)S(1)} %bitcast.113), channel_id=1, replica_groups={{0,2,4,6,8,10,12,14,16,18,20,22,24,26,28,30,32,34,36,38,40,42,44,46,48,..., dimensions={0} | all-to-all | bytes 524288 | tf_op jit(solution)/shard_map/over_plane/all_to_all | solution.py:239
  67.0 35.6 %all_to_all.67 = f32[12,8,512]{2,1,0:T(8,128)S(1)} all-to-all(f32[12,8,512]{2,1,0:T(8,128)S(1)} %broadcast_in_dim.2), channel_id=1, replica_groups=mesh['occ'=12,'tens'=64] {'occ'}, dimensions={0} | all-to-all | bytes 393216 | tf_op jit(solution)/shard_map/over_batches/all_to_all | solution.py:281
  102.6 0.6 broadcast_multiply_fusion
  (3 shorter events, 0.1 us)
Async XLA Ops:
  0.0 3.6 %copy-start = (bf16[768,768]{1,0:T(8,128)(2,1)S(1)}, bf16[768,768]{1,0:T(8,128)(2,1)}, u32[]{:S(2)}) copy-start(bf16[768,768]{1,0:T(8,128)(2,1)} %param.15) | copy-start | bytes 3538948
  0.0 3.6 %copy-start.1 = (bf16[64,768]{1,0:T(8,128)(2,1)S(1)}, bf16[64,768]{1,0:T(8,128)(2,1)}, u32[]{:S(2)}) copy-start(bf16[64,768]{1,0:T(8,128)(2,1)} %param.14) | copy-start | bytes 294916
  0.0 3.6 %copy-start.2 = (s32[12,12]{1,0:T(8,128)S(1)}, s32[12,12]{1,0:T(8,128)}, u32[]{:S(2)}) copy-start(s32[12,12]{1,0:T(8,128)} %mask_hbm.1) | copy-start | bytes 1732
  0.0 3.6 %copy-start.5 = (s32[12,12]{1,0:T(8,128)S(1)}, s32[12,12]{1,0:T(8,128)}, u32[]{:S(2)}) copy-start(s32[12,12]{1,0:T(8,128)} %param.17) | copy-start | bytes 1732
  0.0 3.6 %copy-start.6 = (s32[12,12]{1,0:T(8,128)S(1)}, s32[12,12]{1,0:T(8,128)}, u32[]{:S(2)}) copy-start(s32[12,12]{1,0:T(8,128)} %param.18) | copy-start | bytes 1732
  3.7 25.3 %all-to-all-start = ((bf16[32,8,768]{2,1,0:T(8,128)(2,1)}), bf16[32,8,768]{2,1,0:T(8,128)(2,1)S(1)}, u32[]{:S(2)}, u32[]{:S(2)}) async-start(bf16[32,8,768]{2,1,0:T(8,128)(2,1)} %bitcast), calls=%async_computation | async-start | bytes 786432 | tf_op jit(solution)/shard_map/cond/branch_0_fun/rows/all_to_all | solution.py:239
  29.0 20.7 %all-to-all-start.1 = ((bf16[32,8,768]{2,1,0:T(8,128)(2,1)}), bf16[32,8,768]{2,1,0:T(8,128)(2,1)S(1)}, u32[]{:S(2)}, u32[]{:S(2)}) async-start(bf16[32,8,768]{2,1,0:T(8,128)(2,1)} %bitcast.105), calls=%async_computation.1 | async-start | bytes 786432 | tf_op jit(solution)/shard_map/cond/branch_0_fun/screened/all_to_all | solution.py:239
  34.9 3.6 %collective-permute-start = (bf16[256,768]{1,0:T(8,128)(2,1)S(1)}, bf16[256,768]{1,0:T(8,128)(2,1)S(1)}, u32[]{:S(2)}, u32[]{:S(2)}) collective-permute-start(bf16[256,768]{1,0:T(8,128)(2,1)S(1)} %bitcast.107), channel_id=1, source_target_pairs={{0,1},{1,0},{2,3},{3,2},{4,5},{5,4},{6,7},{7,6},{8,9},{9,8},{10,11... | collective-permute-start | bytes 1179656 | tf_op jit(solution)/shard_map/cond/branch_0_fun/other_rows/ppermute | solution.py:260

commit v6 on v5

--- a/solution.py
+++ b/solution.py
@@ -126,36 +126,42 @@
 
 def screened_kernel(
     batch_ref, mask_ref, tensor_ref, occ_ref, virt_ref, tmask_ref, omask_ref, vmask_ref, out_ref,
-    keep, occ_part, virt_part, occ_half, staged, kept,
+    loaded, keep, occ_part, virt_part, occ_half, staged, kept, arrived,
 ):
-    index = pl.program_id(0)
     local_ri = occ_half.shape[1]
     ao_count = virt_ref.shape[0]
     chips = occ_ref.shape[0] // 2
 
-    @pl.when(index == 0)
-    def _():
-        keep[...] = spread(tmask_ref[...], ao_count, ao_count)
-        virt_part[...] = virt_ref[...] * spread(vmask_ref[...], ao_count, ao_count)
-        pattern = as_bf16(omask_ref[pl.ds(batch_ref[0], 1), :])
-        row_keep = dot_t(pattern, block_of(ao_count, pattern.shape[1])).astype(BF16)
-        occ_part[...] = occ_ref[...] * row_keep
-
-    product = dot(occ_part[...], tensor_ref[0] * keep[...]).astype(BF16)
-    occ_half[0, index] = product[:chips]
-    occ_half[1, index] = product[chips:]
-
-    @pl.when(index == local_ri - 1)
-    def _():
-        count = kept_blocks(batch_ref[0], mask_ref, kept)
-        place = placement(local_ri * chips, local_ri)
-        for half in range(2):
-            values = dot(occ_half[half].reshape(local_ri * chips, ao_count), virt_part[...])
-            ordered = dot(place, values.astype(BF16))
-            for tile in range(ao_count // LANES):
-                staged[half, tile] = ordered[:, tile * LANES : (tile + 1) * LANES]
-        slots = out_ref.shape[1] // LANES
-        gather_blocks(lambda half, tile: staged[half, tile], kept, count, out_ref, 0, slots)
+    def copy(index):
+        return pltpu.make_async_copy(
+            tensor_ref.at[index], loaded.at[index], arrived.at[index]
+        )
+
+    for index in range(local_ri):
+        copy(index).start()
+    keep[...] = spread(tmask_ref[...], ao_count, ao_count)
+    pattern = as_bf16(omask_ref[pl.ds(batch_ref[0], 1), :])
+    row_keep = dot_t(pattern, block_of(ao_count, pattern.shape[1])).astype(BF16)
+    occ_part[...] = occ_ref[...] * row_keep
+    virt_part[...] = virt_ref[...] * spread(vmask_ref[...], ao_count, ao_count)
+
+    def step(index, carry):
+        copy(index).wait()
+        product = dot(occ_part[...], loaded[index] * keep[...]).astype(BF16)
+        occ_half[0, index] = product[:chips]
+        occ_half[1, index] = product[chips:]
+        return carry
+
+    lax.fori_loop(0, local_ri, step, 0)
+    count = kept_blocks(batch_ref[0], mask_ref, kept)
+    place = placement(local_ri * chips, local_ri)
+    for half in range(2):
+        values = dot(occ_half[half].reshape(local_ri * chips, ao_count), virt_part[...])
+        ordered = dot(place, values.astype(BF16))
+        for tile in range(ao_count // LANES):
+            staged[half, tile] = ordered[:, tile * LANES : (tile + 1) * LANES]
+    slots = out_ref.shape[1] // LANES
+    gather_blocks(lambda half, tile: staged[half, tile], kept, count, out_ref, 0, slots)
 
 
 def row_messages(sizes, tensor_mask, tensor, rows):
@@ -189,31 +195,25 @@
     local_ri, ao_count, _ = tensor.shape
     rows = occ_green.shape[0]
     chips = rows // 2
-    whole = lambda s, batch, mask: (0, 0)
-    pattern = pl.BlockSpec(tensor_mask.shape, whole)
+    local = pl.BlockSpec(memory_space=pltpu.VMEM)
     work = local_ri * rows * ao_count * ao_count
     return pl.pallas_call(
         screened_kernel,
         out_shape=jax.ShapeDtypeStruct((chips * local_ri, slots * LANES), BF16),
         grid_spec=pltpu.PrefetchScalarGridSpec(
             num_scalar_prefetch=2,
-            grid=(local_ri,),
-            in_specs=[
-                pl.BlockSpec((1, ao_count, ao_count), lambda s, batch, mask: (s, 0, 0)),
-                pl.BlockSpec(occ_green.shape, whole),
-                pl.BlockSpec(virt_green.shape, whole),
-                pattern,
-                pattern,
-                pattern,
-            ],
-            out_specs=pl.BlockSpec((chips * local_ri, slots * LANES), whole),
+            grid=(),
+            in_specs=[pl.BlockSpec(memory_space=pl.ANY)] + [local] * 5,
+            out_specs=local,
             scratch_shapes=[
+                pltpu.VMEM(tensor.shape, BF16),
                 pltpu.VMEM((ao_count, ao_count), BF16),
                 pltpu.VMEM(occ_green.shape, BF16),
                 pltpu.VMEM(virt_green.shape, BF16),
                 pltpu.VMEM((2, local_ri, chips, ao_count), BF16),
                 pltpu.VMEM((2, ao_count // LANES, chips * local_ri, LANES), F32),
                 pltpu.SMEM((tensor_mask.shape[1] + 1,), jnp.int32),
+                pltpu.SemaphoreType.DMA((local_ri,)),
             ],
         ),
         compiler_params=pltpu.CompilerParams(vmem_limit_bytes=56 * 2**20),

time: 104 us -> 97.9 us (0.941)
  blocking collectives: 51.7 us -> 48 us
  Pallas kernels: 14.4 us -> 10.7 us
  waiting for transfers between devices: 16.8 us -> 20.1 us
  starting transfers between devices: 17.7 us -> 16.1 us
    all_to_all x1, blocking collectives: 35.6 us -> 31.7 us  [body(): batch_shares = lax.all_to_all(copies, 'occ', 0, 0, tiled=True)]
    pallas_call x1, Pallas kernels: 11.4 us -> 7.76 us  [screened_messages(): pl.pallas_call(screened_kernel, out_shape=jax.ShapeDtypeStruct((chips * l...]
    all_to_all x2, waiting for transfers between devices: 15.1 us -> 18.5 us  [over_plane(): lax.all_to_all(values, 'tens', 0, 0, axis_index_groups=same_core, tiled=T...]
    all_to_all x2, starting transfers between devices: 15.8 us -> 14.2 us  [over_plane(): lax.all_to_all(values, 'tens', 0, 0, axis_index_groups=same_core, tiled=T...]
  transfers between devices with their start and end apart: 3 -> 3, of which waited for: 3 -> 3; matrix products, arithmetic and copies ran while one was open for 0% -> 0% of each run, Pallas kernels for 11% -> 8%
where the time goes in v6:
time: 97.9 us; the launch traced here: 97.4 us
  blocking collectives  48 us (49%)
  waiting for transfers between devices  20.1 us (21%)
  starting transfers between devices  16.1 us (16%)
  Pallas kernels  10.7 us (11%)
    all_to_all x1, blocking collectives, body(): batch_shares = lax.all_to_all(copies, 'occ', 0, 0, tiled=True)  31.7 us
    all_to_all x2, waiting for transfers between devices, over_plane(): lax.all_to_all(values, 'tens', 0, 0, axis_index_groups=same_core, tiled=T...  18.5 us
    all_to_all x1, blocking collectives, over_plane(): lax.all_to_all(values, 'tens', 0, 0, axis_index_groups=same_core, tiled=T...  16.3 us
    all_to_all x2, starting transfers between devices, over_plane(): lax.all_to_all(values, 'tens', 0, 0, axis_index_groups=same_core, tiled=T...  14.2 us
    pallas_call x1, Pallas kernels, screened_messages(): pl.pallas_call(screened_kernel, out_shape=jax.ShapeDtypeStruct((chips * l...  7.76 us
    pallas_call x1, Pallas kernels, row_messages(): pl.pallas_call(functools.partial(rows_kernel, sizes), out_shape=(*shapes,...  2.93 us
  transfers between devices with their start and end apart: 3, of which 3 were waited for; matrix products, arithmetic and copies ran while one was open for 0% of the time, Pallas kernels for 8%

profile of v6, /device:TPU:64, one launch (start us, length us, event | category | flops | bytes accessed | tf_op | source)
XLA Modules:
  0.0 97.4 jit_solution(13283609407315816599)
XLA Ops:
  0.0 0.0 copy-start
  0.0 0.0 copy-start.1
  0.0 0.0 copy-start.2
  0.0 0.0 copy-start.5
  0.0 0.0 copy-start.6
  0.0 2.9 %row_messages.1 = (bf16[256,768]{1,0:T(8,128)(2,1)}, bf16[256,896]{1,0:T(8,128)(2,1)}, bf16[256,1024]{1,0:T(8,128)(2,1)}, bf16[256,1152]{1,0:T(8,128)(2,1)}, bf1...) custom-call(s32[12,12]{1,0:T(8,128)} %mask_hbm.1, ...), custom_call_target="tpu_custom_call" | custom-call | tf_op jit(solution)/shard_map/row_messages/pallas_call | solution.py:172
  3.6 0.0 copy-done
  3.6 0.0 copy-done.1
  3.6 0.0 copy-done.2
  3.6 0.0 copy-done.5
  3.7 0.0 copy-done.6
  3.7 45.1 %conditional.2 = (bf16[256,512]{1,0:T(8,128)(2,1)S(1)}) conditional(s32[]{:T(128)} %bitcast.49, (bf16[256,768]{1,0:T(8,128)(2,1)}, s32[1]{0:T(128)}, s32[12,12]{1,0:T(8,128)S(1)}, bf16[8,768,768]{2,1,0:T(8,128)(2,1)}, bf16[64,768]{1,0:T(8,128)(2,1)S(1)}, /*index=5*/bf16[768,768]{1,0:T(8,128)(2,1)S(1)}, ...), branch_computations={%region_0.1_spmd, %region_1.2_spmd, %region_2.3_spmd, %region_3.4_... | conditional | flops 1612185600 | bytes 31719572
  3.7 10.0 %all-to-all-start = ((bf16[32,8,768]{2,1,0:T(8,128)(2,1)}), bf16[32,8,768]{2,1,0:T(8,128)(2,1)S(1)}, u32[]{:S(2)}, u32[]{:S(2)}) async-start(bf16[32,8,768]{2,1,0:T(8,128)(2,1)} %bitcast), calls=%async_computation | async-start | bytes 786432 | tf_op jit(solution)/shard_map/cond/branch_0_fun/rows/all_to_all | solution.py:239
  13.7 7.8 %screened_messages.7 = bf16[256,768]{1,0:T(8,128)(2,1)} custom-call(s32[1]{0:T(128)} %get-tuple-element.140.batch_ref, s32[12,12]{1,0:T(8,128)S(1)} %get-tuple-element.142.mask_ref.tmask_ref, bf16[8,768,768]{2,1,0:T(8,128)(2,1)} %get-tuple-element.144.tensor_ref, bf16[64,768]{1,0:T(8,128)(2,1)S(1)} %get-tuple-element.145.occ_ref, ...), custom_call_target="tpu_custom_call" | custom-call | flops 1207959552 | bytes 11796480 | tf_op jit(solution)/shard_map/cond/branch_0_fun/screened_messages/pallas_call | solution.py:200
  21.4 7.6 %all-to-all-done = bf16[32,8,768]{2,1,0:T(8,128)(2,1)S(1)} async-done(((bf16[32,8,768]{2,1,0:T(8,128)(2,1)}), bf16[32,8,768]{2,1,0:T(8,128)(2,1)S(1)}, u32[]{:S(2)}, u32[]{:S(2)}) %all-to-all-start) | async-done | bytes 393248 | tf_op jit(solution)/shard_map/cond/branch_0_fun/rows/all_to_all | solution.py:239
  29.0 4.2 %all-to-all-start.1 = ((bf16[32,8,768]{2,1,0:T(8,128)(2,1)}), bf16[32,8,768]{2,1,0:T(8,128)(2,1)S(1)}, u32[]{:S(2)}, u32[]{:S(2)}) async-start(bf16[32,8,768]{2,1,0:T(8,128)(2,1)} %bitcast.105), calls=%async_computation.1 | async-start | bytes 786432 | tf_op jit(solution)/shard_map/cond/branch_0_fun/screened/all_to_all | solution.py:239
  33.3 1.9 %collective-permute-start = (bf16[256,768]{1,0:T(8,128)(2,1)S(1)}, bf16[256,768]{1,0:T(8,128)(2,1)S(1)}, u32[]{:S(2)}, u32[]{:S(2)}) collective-permute-start(bf16[256,768]{1,0:T(8,128)(2,1)S(1)} %bitcast.107), channel_id=1, source_target_pairs={{0,1},{1,0},{2,3},{3,2},{4,5},{5,4},{6,7},{7,6},{8,9},{9,8},{10,11... | collective-permute-start | bytes 1179656 | tf_op jit(solution)/shard_map/cond/branch_0_fun/other_rows/ppermute | solution.py:260
  35.2 1.7 %collective-permute-done = bf16[256,768]{1,0:T(8,128)(2,1)S(1)} collective-permute-done((bf16[256,768]{1,0:T(8,128)(2,1)S(1)}, bf16[256,768]{1,0:T(8,128)(2,1)S(1)}, u32[]{:S(2)}, u32[]{:S(2)}) %collective-permute-start) | collective-permute-done | bytes 393248 | tf_op jit(solution)/shard_map/cond/branch_0_fun/other_rows/ppermute | solution.py:260
  36.9 10.9 %all-to-all-done.1 = bf16[32,8,768]{2,1,0:T(8,128)(2,1)S(1)} async-done(((bf16[32,8,768]{2,1,0:T(8,128)(2,1)}), bf16[32,8,768]{2,1,0:T(8,128)(2,1)S(1)}, u32[]{:S(2)}, u32[]{:S(2)}) %all-to-all-start.1) | async-done | bytes 393248 | tf_op jit(solution)/shard_map/cond/branch_0_fun/screened/all_to_all | solution.py:239
  47.7 0.1 select_bitcast_fusion.1
  47.8 0.1 pad_maximum_fusion
  47.9 0.4 fusion
  48.7 16.3 %all_to_all.66 = bf16[32,8,512]{2,1,0:T(8,128)(2,1)S(1)} all-to-all(bf16[32,8,512]{2,1,0:T(8,128)(2,1)S(1)} %bitcast.113), channel_id=1, replica_groups={{0,2,4,6,8,10,12,14,16,18,20,22,24,26,28,30,32,34,36,38,40,42,44,46,48,..., dimensions={0} | all-to-all | bytes 524288 | tf_op jit(solution)/shard_map/over_plane/all_to_all | solution.py:239
  65.1 31.7 %all_to_all.67 = f32[12,8,512]{2,1,0:T(8,128)S(1)} all-to-all(f32[12,8,512]{2,1,0:T(8,128)S(1)} %broadcast_in_dim.2), channel_id=1, replica_groups=mesh['occ'=12,'tens'=64] {'occ'}, dimensions={0} | all-to-all | bytes 393216 | tf_op jit(solution)/shard_map/over_batches/all_to_all | solution.py:281
  96.8 0.6 broadcast_multiply_fusion
  (3 shorter events, 0.1 us)
Async XLA Ops:
  0.0 3.6 %copy-start = (bf16[768,768]{1,0:T(8,128)(2,1)S(1)}, bf16[768,768]{1,0:T(8,128)(2,1)}, u32[]{:S(2)}) copy-start(bf16[768,768]{1,0:T(8,128)(2,1)} %param.15) | copy-start | bytes 3538948
  0.0 3.6 %copy-start.1 = (bf16[64,768]{1,0:T(8,128)(2,1)S(1)}, bf16[64,768]{1,0:T(8,128)(2,1)}, u32[]{:S(2)}) copy-start(bf16[64,768]{1,0:T(8,128)(2,1)} %param.14) | copy-start | bytes 294916
  0.0 3.6 %copy-start.2 = (s32[12,12]{1,0:T(8,128)S(1)}, s32[12,12]{1,0:T(8,128)}, u32[]{:S(2)}) copy-start(s32[12,12]{1,0:T(8,128)} %mask_hbm.1) | copy-start | bytes 1732
  0.0 3.6 %copy-start.5 = (s32[12,12]{1,0:T(8,128)S(1)}, s32[12,12]{1,0:T(8,128)}, u32[]{:S(2)}) copy-start(s32[12,12]{1,0:T(8,128)} %param.17) | copy-start | bytes 1732
  0.0 3.6 %copy-start.6 = (s32[12,12]{1,0:T(8,128)S(1)}, s32[12,12]{1,0:T(8,128)}, u32[]{:S(2)}) copy-start(s32[12,12]{1,0:T(8,128)} %param.18) | copy-start | bytes 1732
  3.7 25.3 %all-to-all-start = ((bf16[32,8,768]{2,1,0:T(8,128)(2,1)}), bf16[32,8,768]{2,1,0:T(8,128)(2,1)S(1)}, u32[]{:S(2)}, u32[]{:S(2)}) async-start(bf16[32,8,768]{2,1,0:T(8,128)(2,1)} %bitcast), calls=%async_computation | async-start | bytes 786432 | tf_op jit(solution)/shard_map/cond/branch_0_fun/rows/all_to_all | solution.py:239
  29.0 18.7 %all-to-all-start.1 = ((bf16[32,8,768]{2,1,0:T(8,128)(2,1)}), bf16[32,8,768]{2,1,0:T(8,128)(2,1)S(1)}, u32[]{:S(2)}, u32[]{:S(2)}) async-start(bf16[32,8,768]{2,1,0:T(8,128)(2,1)} %bitcast.105), calls=%async_computation.1 | async-start | bytes 786432 | tf_op jit(solution)/shard_map/cond/branch_0_fun/screened/all_to_all | solution.py:239
  33.3 3.6 %collective-permute-start = (bf16[256,768]{1,0:T(8,128)(2,1)S(1)}, bf16[256,768]{1,0:T(8,128)(2,1)S(1)}, u32[]{:S(2)}, u32[]{:S(2)}) collective-permute-start(bf16[256,768]{1,0:T(8,128)(2,1)S(1)} %bitcast.107), channel_id=1, source_target_pairs={{0,1},{1,0},{2,3},{3,2},{4,5},{5,4},{6,7},{7,6},{8,9},{9,8},{10,11... | collective-permute-start | bytes 1179656 | tf_op jit(solution)/shard_map/cond/branch_0_fun/other_rows/ppermute | solution.py:260

commit v7 on v6

--- a/solution.py
+++ b/solution.py
@@ -276,10 +276,10 @@
     with jax.named_scope("over_plane"):
         shares = over_plane(partial_value.reshape(chips, local_ri, -1))
     batch_share = jnp.sum(shares.astype(F32), axis=0)
-    copies = jnp.broadcast_to(batch_share[None], (batches,) + batch_share.shape)
+    copies = jnp.broadcast_to(batch_share.astype(BF16)[None], (batches,) + batch_share.shape)
     with jax.named_scope("over_batches"):
         batch_shares = lax.all_to_all(copies, "occ", 0, 0, tiled=True)
-    return jnp.sum(batch_shares, axis=0) * (-1.0 / ao_count)
+    return jnp.sum(batch_shares.astype(F32), axis=0) * (-1.0 / ao_count)
 
 
 def solution(mesh):

time: 97.9 us -> 96.3 us (0.984)
  the two profiles are of different devices: /device:TPU:64 before, /device:TPU:8 now
where the time goes in v7:
time: 96.3 us; the launch traced here: 97.4 us
  blocking collectives  49.5 us (51%)
  starting transfers between devices  20.5 us (21%)
  waiting for transfers between devices  14.2 us (15%)
  Pallas kernels  10.7 us (11%)
    all_to_all x1, blocking collectives, body(): batch_shares = lax.all_to_all(copies, 'occ', 0, 0, tiled=True)  33.9 us
    all_to_all x2, starting transfers between devices, over_plane(): lax.all_to_all(values, 'tens', 0, 0, axis_index_groups=same_core, tiled=T...  18.6 us
    all_to_all x1, blocking collectives, over_plane(): lax.all_to_all(values, 'tens', 0, 0, axis_index_groups=same_core, tiled=T...  15.5 us
    all_to_all x2, waiting for transfers between devices, over_plane(): lax.all_to_all(values, 'tens', 0, 0, axis_index_groups=same_core, tiled=T...  12.5 us
    pallas_call x1, Pallas kernels, screened_messages(): pl.pallas_call(screened_kernel, out_shape=jax.ShapeDtypeStruct((chips * l...  7.76 us
    pallas_call x1, Pallas kernels, row_messages(): pl.pallas_call(functools.partial(rows_kernel, sizes), out_shape=(*shapes,...  2.93 us
  transfers between devices with their start and end apart: 3, of which 3 were waited for; matrix products, arithmetic and copies ran while one was open for 0% of the time, Pallas kernels for 8%

profile of v7, /device:TPU:8, one launch (start us, length us, event | category | flops | bytes accessed | tf_op | source)
XLA Modules:
  0.0 97.4 jit_solution(14747213004175107505)
XLA Ops:
  0.0 0.0 copy-start
  0.0 0.0 copy-start.1
  0.0 0.0 copy-start.2
  0.0 0.0 copy-start.5
  0.0 0.0 copy-start.6
  0.0 2.9 %row_messages.1 = (bf16[256,768]{1,0:T(8,128)(2,1)}, bf16[256,896]{1,0:T(8,128)(2,1)}, bf16[256,1024]{1,0:T(8,128)(2,1)}, bf16[256,1152]{1,0:T(8,128)(2,1)}, bf1...) custom-call(s32[12,12]{1,0:T(8,128)} %mask_hbm.1, ...), custom_call_target="tpu_custom_call" | custom-call | tf_op jit(solution)/shard_map/row_messages/pallas_call | solution.py:172
  3.6 0.0 copy-done
  3.6 0.0 copy-done.1
  3.6 0.0 copy-done.2
  3.7 0.0 copy-done.5
  3.7 0.0 copy-done.6
  3.7 43.5 %conditional.2 = (bf16[256,512]{1,0:T(8,128)(2,1)S(1)}) conditional(s32[]{:T(128)} %bitcast.49, (bf16[256,768]{1,0:T(8,128)(2,1)}, s32[1]{0:T(128)}, s32[12,12]{1,0:T(8,128)S(1)}, bf16[8,768,768]{2,1,0:T(8,128)(2,1)}, bf16[64,768]{1,0:T(8,128)(2,1)S(1)}, /*index=5*/bf16[768,768]{1,0:T(8,128)(2,1)S(1)}, ...), branch_computations={%region_0.1_spmd, %region_1.2_spmd, %region_2.3_spmd, %region_3.4_... | conditional | flops 1612185600 | bytes 31719572
  3.7 13.0 %all-to-all-start = ((bf16[32,8,768]{2,1,0:T(8,128)(2,1)}), bf16[32,8,768]{2,1,0:T(8,128)(2,1)S(1)}, u32[]{:S(2)}, u32[]{:S(2)}) async-start(bf16[32,8,768]{2,1,0:T(8,128)(2,1)} %bitcast), calls=%async_computation | async-start | bytes 786432 | tf_op jit(solution)/shard_map/cond/branch_0_fun/rows/all_to_all | solution.py:239
  16.7 7.8 %screened_messages.7 = bf16[256,768]{1,0:T(8,128)(2,1)} custom-call(s32[1]{0:T(128)} %get-tuple-element.140.batch_ref, s32[12,12]{1,0:T(8,128)S(1)} %get-tuple-element.142.mask_ref.tmask_ref, bf16[8,768,768]{2,1,0:T(8,128)(2,1)} %get-tuple-element.144.tensor_ref, bf16[64,768]{1,0:T(8,128)(2,1)S(1)} %get-tuple-element.145.occ_ref, ...), custom_call_target="tpu_custom_call" | custom-call | flops 1207959552 | bytes 11796480 | tf_op jit(solution)/shard_map/cond/branch_0_fun/screened_messages/pallas_call | solution.py:200
  24.5 4.3 %all-to-all-done = bf16[32,8,768]{2,1,0:T(8,128)(2,1)S(1)} async-done(((bf16[32,8,768]{2,1,0:T(8,128)(2,1)}), bf16[32,8,768]{2,1,0:T(8,128)(2,1)S(1)}, u32[]{:S(2)}, u32[]{:S(2)}) %all-to-all-start) | async-done | bytes 393248 | tf_op jit(solution)/shard_map/cond/branch_0_fun/rows/all_to_all | solution.py:239
  28.7 5.6 %all-to-all-start.1 = ((bf16[32,8,768]{2,1,0:T(8,128)(2,1)}), bf16[32,8,768]{2,1,0:T(8,128)(2,1)S(1)}, u32[]{:S(2)}, u32[]{:S(2)}) async-start(bf16[32,8,768]{2,1,0:T(8,128)(2,1)} %bitcast.105), calls=%async_computation.1 | async-start | bytes 786432 | tf_op jit(solution)/shard_map/cond/branch_0_fun/screened/all_to_all | solution.py:239
  34.4 1.9 %collective-permute-start = (bf16[256,768]{1,0:T(8,128)(2,1)S(1)}, bf16[256,768]{1,0:T(8,128)(2,1)S(1)}, u32[]{:S(2)}, u32[]{:S(2)}) collective-permute-start(bf16[256,768]{1,0:T(8,128)(2,1)S(1)} %bitcast.107), channel_id=1, source_target_pairs={{0,1},{1,0},{2,3},{3,2},{4,5},{5,4},{6,7},{7,6},{8,9},{9,8},{10,11... | collective-permute-start | bytes 1179656 | tf_op jit(solution)/shard_map/cond/branch_0_fun/other_rows/ppermute | solution.py:260
  36.3 1.7 %collective-permute-done = bf16[256,768]{1,0:T(8,128)(2,1)S(1)} collective-permute-done((bf16[256,768]{1,0:T(8,128)(2,1)S(1)}, bf16[256,768]{1,0:T(8,128)(2,1)S(1)}, u32[]{:S(2)}, u32[]{:S(2)}) %collective-permute-start) | collective-permute-done | bytes 393248 | tf_op jit(solution)/shard_map/cond/branch_0_fun/other_rows/ppermute | solution.py:260
  38.0 8.2 %all-to-all-done.1 = bf16[32,8,768]{2,1,0:T(8,128)(2,1)S(1)} async-done(((bf16[32,8,768]{2,1,0:T(8,128)(2,1)}), bf16[32,8,768]{2,1,0:T(8,128)(2,1)S(1)}, u32[]{:S(2)}, u32[]{:S(2)}) %all-to-all-start.1) | async-done | bytes 393248 | tf_op jit(solution)/shard_map/cond/branch_0_fun/screened/all_to_all | solution.py:239
  46.2 0.1 select_bitcast_fusion.1
  46.3 0.1 pad_maximum_fusion
  46.4 0.4 fusion
  47.2 15.5 %all_to_all.66 = bf16[32,8,512]{2,1,0:T(8,128)(2,1)S(1)} all-to-all(bf16[32,8,512]{2,1,0:T(8,128)(2,1)S(1)} %bitcast.113), channel_id=1, replica_groups={{0,2,4,6,8,10,12,14,16,18,20,22,24,26,28,30,32,34,36,38,40,42,44,46,48,..., dimensions={0} | all-to-all | bytes 524288 | tf_op jit(solution)/shard_map/over_plane/all_to_all | solution.py:239
  62.7 0.1 reduce_sum.21
  62.8 33.9 %all_to_all.67 = bf16[12,8,512]{2,1,0:T(8,128)(2,1)S(1)} all-to-all(bf16[12,8,512]{2,1,0:T(8,128)(2,1)S(1)} %broadcast_in_dim.2), channel_id=1, replica_groups=mesh['occ'=12,'tens'=64] {'occ'}, dimensions={0} | all-to-all | bytes 196608 | tf_op jit(solution)/shard_map/over_batches/all_to_all | solution.py:281
  96.8 0.6 broadcast_multiply_fusion
  (2 shorter events, 0.0 us)
Async XLA Ops:
  0.0 3.6 %copy-start = (bf16[768,768]{1,0:T(8,128)(2,1)S(1)}, bf16[768,768]{1,0:T(8,128)(2,1)}, u32[]{:S(2)}) copy-start(bf16[768,768]{1,0:T(8,128)(2,1)} %param.15) | copy-start | bytes 3538948
  0.0 3.6 %copy-start.1 = (bf16[64,768]{1,0:T(8,128)(2,1)S(1)}, bf16[64,768]{1,0:T(8,128)(2,1)}, u32[]{:S(2)}) copy-start(bf16[64,768]{1,0:T(8,128)(2,1)} %param.14) | copy-start | bytes 294916
  0.0 3.6 %copy-start.2 = (s32[12,12]{1,0:T(8,128)S(1)}, s32[12,12]{1,0:T(8,128)}, u32[]{:S(2)}) copy-start(s32[12,12]{1,0:T(8,128)} %mask_hbm.1) | copy-start | bytes 1732
  0.0 3.6 %copy-start.5 = (s32[12,12]{1,0:T(8,128)S(1)}, s32[12,12]{1,0:T(8,128)}, u32[]{:S(2)}) copy-start(s32[12,12]{1,0:T(8,128)} %param.17) | copy-start | bytes 1732
  0.0 3.6 %copy-start.6 = (s32[12,12]{1,0:T(8,128)S(1)}, s32[12,12]{1,0:T(8,128)}, u32[]{:S(2)}) copy-start(s32[12,12]{1,0:T(8,128)} %param.18) | copy-start | bytes 1732
  3.7 25.0 %all-to-all-start = ((bf16[32,8,768]{2,1,0:T(8,128)(2,1)}), bf16[32,8,768]{2,1,0:T(8,128)(2,1)S(1)}, u32[]{:S(2)}, u32[]{:S(2)}) async-start(bf16[32,8,768]{2,1,0:T(8,128)(2,1)} %bitcast), calls=%async_computation | async-start | bytes 786432 | tf_op jit(solution)/shard_map/cond/branch_0_fun/rows/all_to_all | solution.py:239
  28.7 17.5 %all-to-all-start.1 = ((bf16[32,8,768]{2,1,0:T(8,128)(2,1)}), bf16[32,8,768]{2,1,0:T(8,128)(2,1)S(1)}, u32[]{:S(2)}, u32[]{:S(2)}) async-start(bf16[32,8,768]{2,1,0:T(8,128)(2,1)} %bitcast.105), calls=%async_computation.1 | async-start | bytes 786432 | tf_op jit(solution)/shard_map/cond/branch_0_fun/screened/all_to_all | solution.py:239
  34.4 3.6 %collective-permute-start = (bf16[256,768]{1,0:T(8,128)(2,1)S(1)}, bf16[256,768]{1,0:T(8,128)(2,1)S(1)}, u32[]{:S(2)}, u32[]{:S(2)}) collective-permute-start(bf16[256,768]{1,0:T(8,128)(2,1)S(1)} %bitcast.107), channel_id=1, source_target_pairs={{0,1},{1,0},{2,3},{3,2},{4,5},{5,4},{6,7},{7,6},{8,9},{9,8},{10,11... | collective-permute-start | bytes 1179656 | tf_op jit(solution)/shard_map/cond/branch_0_fun/other_rows/ppermute | solution.py:260
